TPU v7x, 128 devices: a whole 4x4x4 slice. The times are simulated.
128 devices in a mesh: ctx: 32 (over x, z, y_hi), fsdp: 4 (over y_lo, core).
Axes of the slice: x: 4, y: 4 (y_hi: 2, y_lo: 2; y = y_hi * 2 + y_lo), z: 4, core: 2. Of those that a mesh axis runs over, the one named last changes fastest.
Arguments:
- block_input: bfloat16 [4, 4096, 1024], P('fsdp', 'ctx'), may hold values from -6 to 6
- routes: int32 [4, 4096, 8], P('fsdp', 'ctx'), may hold values from 0 to 31, all different within a row; in each aligned block of 128 rows (0 to 127, 128 to 255, ..., all dimensions but the last counted through in order) at most 48 rows name the same one
- block_pairs: int32 [32], replicated, may hold values from 0 to 31, each once
- norm1_gain: bfloat16 [1024], P('fsdp'), may hold values from 0.5 to 1.5
- w_query: bfloat16 [1024, 1024], P('fsdp'), may hold values from -0.75 to 0.75
- w_key: bfloat16 [1024, 512], P('fsdp'), may hold values from -0.75 to 0.75
- w_value: bfloat16 [1024, 512], P('fsdp'), may hold values from -0.1875 to 0.1875
- w_out: bfloat16 [1024, 1024], P('fsdp'), may hold values from -4 to 4
- norm2_gain: bfloat16 [1024], P('fsdp'), may hold values from 0.5 to 1.5
- w_router: bfloat16 [1024, 32], P('fsdp'), may hold values from -0.09375 to 0.09375
- w_gate: bfloat16 [32, 1024, 512], P('ctx', 'fsdp'), may hold values from -0.1875 to 0.1875
- w_up: bfloat16 [32, 1024, 512], P('ctx', 'fsdp'), may hold values from -0.1875 to 0.1875
- w_down: bfloat16 [32, 512, 1024], P('ctx', 'fsdp'), may hold values from -4 to 4
- cotangent: bfloat16 [4, 4096, 1024], P('fsdp', 'ctx'), may hold values from -6 to 6
Outputs:
- block_output: bfloat16 [4, 4096, 1024], P('fsdp', 'ctx')
- input_grad: float32 [4, 4096, 1024], P('fsdp', 'ctx')
- norm1_gain_grad: float32 [1024], P('fsdp')
- w_query_grad: float32 [1024, 1024], P('fsdp')
- w_key_grad: float32 [1024, 512], P('fsdp')
- w_value_grad: float32 [1024, 512], P('fsdp')
- w_out_grad: float32 [1024, 1024], P('fsdp')
- norm2_gain_grad: float32 [1024], P('fsdp')
- w_router_grad: float32 [1024, 32], P('fsdp')
- w_gate_grad: float32 [32, 1024, 512], P('ctx', 'fsdp')
- w_up_grad: float32 [32, 1024, 512], P('ctx', 'fsdp')
- w_down_grad: float32 [32, 512, 1024], P('ctx', 'fsdp')
Inputs may be any that keep to these rules, and one draw needn't show every extreme that they name: `routes`: each row names 8 different experts; among the 128 rows of one device no expert is named more than 48 times, a bound that some block reaches. `block_pairs`: each number appears once. Index c of ctx holds, in this order, the blocks of half of 128 tokens numbered block_pairs[c] and 63 - block_pairs[c].
All inputs are finite; a program needn't handle non-finite values.
Results may differ from a plain program's by a relative error of at most 0.035.
Values may be sent and summed in bfloat16 or wider, within the bound.
No kernel may reach another device: no remote copies, remote signals or barrier semaphores. Data moves between devices by JAX's collectives and lax.ppermute only.
A program may use at most 128 MiB of HBM per device.

v0:
```python
import functools

import jax
import jax.numpy as jnp
from jax import lax
from jax.experimental import pallas as pl
from jax.experimental.layout import Layout, with_layout_constraint
from jax.experimental.pallas import tpu as pltpu
from jax.sharding import Mesh
from jax.sharding import PartitionSpec as P

HEADS = 16
KV_HEADS = 8
HEAD_DIM = 64
EXPERTS = 32
TOP = 8
CAP = 48
HALF = 64
TILE = 512

epsilon = 1e-06
attn_scale = 0.015625
residual_scale = 0.22
masked_value = -1e30

CTX = ("x", "z", "yh")
ZY = ("z", "yh")
EVERY = ("x", "z", "yh", "yl", "core")
bf16 = jnp.bfloat16
f32 = jnp.float32


def product(left, right):
    return jnp.dot(left, right, preferred_element_type=f32)


def product_nt(left, right):
    return lax.dot_general(left, right, (((1,), (1,)), ((), ())), preferred_element_type=f32)


def product_tn(left, right):
    return lax.dot_general(left, right, (((0,), (0,)), ((), ())), preferred_element_type=f32)


def swap(values, axis):
    return lax.ppermute(values, axis, [(0, 1), (1, 0)])


def turn(values, axis, step):
    return lax.ppermute(values, axis, [(i, (i + step) % 4) for i in range(4)])


def rows_first(values):
    return with_layout_constraint(values, Layout(major_to_minor=tuple(range(values.ndim))))


def exchange(values, axes):
    return rows_first(lax.all_to_all(rows_first(values), axes, 0, 0, tiled=True))


def tie(values, *others):
    if values.size <= 1024:
        return values + sum(other[(0,) * other.ndim].astype(f32) * 0.0 for other in others).astype(values.dtype)
    corner = tuple(slice(0, min(size, 8 if axis < values.ndim - 1 else 128)) for axis, size in enumerate(values.shape))
    nothing = sum(other[(0,) * other.ndim].astype(f32) * 0.0 for other in others)
    held = values[corner] + nothing.astype(values.dtype)
    return lax.dynamic_update_slice(values, held, (0,) * values.ndim)


def pieces_direct(shard):
    steps = [lax.ppermute(shard, ("yl", "core"), [(i, i ^ k) for i in range(4)]) for k in (1, 2, 3)]
    return (shard, *steps)


def pieces_by_row(shard, other):
    return (shard, swap(shard, "core"), other, swap(other, "core"))


def scatter_core(parts):
    core = lax.axis_index("core")
    parts = parts.astype(bf16).reshape((2, 2) + parts.shape[1:])
    away = lax.dynamic_index_in_dim(parts, 1 - core, 1, keepdims=False)
    keep = lax.dynamic_index_in_dim(parts, core, 1, keepdims=False)
    return (keep.astype(f32) + swap(away, "core").astype(f32)).astype(bf16)


def join_core(keep, away):
    return (keep.astype(f32) + swap(away, "core").astype(f32)).astype(bf16)


def scatter_row(both):
    row = lax.axis_index("yl")
    away = lax.dynamic_index_in_dim(both, 1 - row, 0, keepdims=False)
    keep = lax.dynamic_index_in_dim(both, row, 0, keepdims=False)
    return keep.astype(f32) + swap(away, "yl").astype(f32)


def scatter_fsdp(parts):
    return scatter_row(scatter_core(parts))


def all_x(part):
    return [part] + [turn(part, "x", step) for step in (1, 2, 3)]


def rope_tables(positions):
    freqs = jnp.power(10000.0, -jnp.arange(0, HEAD_DIM, 2, dtype=f32) / HEAD_DIM)
    angles = positions.astype(f32)[:, None] * freqs[None, :]
    cosine, sine = jnp.cos(angles), jnp.sin(angles)
    ones, zeros = jnp.ones_like(cosine), jnp.zeros_like(cosine)
    return (
        jnp.concatenate([cosine] * 6 + [ones] * 2, axis=1),
        jnp.concatenate([-sine, sine] * 3 + [zeros] * 2, axis=1),
    )


def turned(values):
    width = values.shape[1]
    column = lax.broadcasted_iota(jnp.int32, values.shape, 1)
    return jnp.where(
        column % HEAD_DIM < HEAD_DIM // 2,
        pltpu.roll(values, width - HEAD_DIM // 2, 1),
        pltpu.roll(values, HEAD_DIM // 2, 1),
    )


def norm_back(values, inv_rms, gain, grad):
    weighted = grad * gain
    gain_grad = jnp.sum(grad * values * inv_rms, axis=0, keepdims=True)
    inner_mean = jnp.mean(weighted * values, axis=-1, keepdims=True)
    return (weighted * inv_rms - values * inv_rms * inv_rms * inv_rms * inner_mean, gain_grad)


def inv_rms_of(values):
    return lax.rsqrt(jnp.mean(values * values, axis=-1, keepdims=True) + epsilon)


def half(index):
    return pl.ds(pl.multiple_of(index * HALF, HALF), HALF)


def key_tile(counter):
    return pl.ds(pl.multiple_of(counter * TILE, TILE), TILE)


def sort_keys(knum_ref, kv_refs, kvs, kvt):
    blocks = kv_refs[0].shape[0] // HALF
    for slot, kv_ref in enumerate(kv_refs):
        for block in range(blocks):
            kvs[half(knum_ref[slot * blocks + block]), :] = kv_ref[block * HALF : (block + 1) * HALF, :]
    for tile in range(kvs.shape[0] // TILE):
        part = kvs[tile * TILE : (tile + 1) * TILE, :].astype(f32)
        kvt[:, tile * TILE : (tile + 1) * TILE] = part.T.astype(bf16)


def pair_rows(ref, first, second, upper):
    rows = []
    for block in (first, second):
        values = ref[half(block), :].astype(f32)
        column = lax.broadcasted_iota(jnp.int32, values.shape, 1)
        inside = (column >= HEAD_DIM) if upper else (column < HEAD_DIM)
        moved = pltpu.roll(values, HEAD_DIM, 1)
        heads = (moved, values) if upper else (values, moved)
        rows += [jnp.where(inside, head, 0.0) for head in heads]
    return jnp.concatenate(rows, axis=0)


def pair_positions(low_number, high_number):
    column = lax.broadcasted_iota(jnp.int32, (1, 4 * HALF), 1)
    return jnp.where(column < 2 * HALF, low_number, high_number) * HALF + column % HALF


def score_tile(keys, queries, counter, positions, masked):
    scores = product_nt(keys, queries)
    if masked:
        key_pos = counter * TILE + lax.broadcasted_iota(jnp.int32, scores.shape, 0)
        scores = jnp.where(key_pos <= positions, scores, masked_value)
    return scores


def store_rows(ref, turned, first, second):
    rows = turned.T
    ref[half(first), :] = jnp.concatenate([rows[:HALF], rows[HALF : 2 * HALF]], axis=1).astype(ref.dtype)
    ref[half(second), :] = jnp.concatenate([rows[2 * HALF : 3 * HALF], rows[3 * HALF :]], axis=1).astype(ref.dtype)


def attend_kernel(
    order_ref, qnum_ref, knum_ref, q_ref, kv0, kv1, kv2, kv3, out_ref, turned_ref, lse_ref, kvs, kvt
):
    sort_keys(knum_ref, (kv0, kv1, kv2, kv3), kvs, kvt)
    width = 4 * HALF

    @pl.loop(0, q_ref.shape[0] // (2 * HALF))
    def _(pair):
        first, second = order_ref[2 * pair], order_ref[2 * pair + 1]
        low_number, high_number = qnum_ref[first], qnum_ref[second]
        queries = pair_rows(q_ref, first, second, False).astype(bf16)
        positions = pair_positions(low_number, high_number)

        def step(masked, counter, running):
            top, total, mixed = running
            scores = score_tile(kvs[key_tile(counter), :], queries, counter, positions, masked)
            new_top = jnp.maximum(top, jnp.max(scores, axis=0, keepdims=True))
            probs = jnp.exp(scores - new_top)
            shrink = jnp.exp(top - new_top)
            total = total * shrink + jnp.sum(probs, axis=0, keepdims=True)
            mixed = mixed * shrink + product(kvt[HEAD_DIM:, key_tile(counter)], probs.astype(bf16))
            return (new_top, total, mixed)

        start = (
            jnp.full((1, width), masked_value, f32),
            jnp.zeros((1, width), f32),
            jnp.zeros((HEAD_DIM, width), f32),
        )
        full = (low_number * HALF) // TILE
        last = (high_number * HALF) // TILE + 1
        running = lax.fori_loop(0, full, functools.partial(step, False), start)
        top, total, mixed = lax.fori_loop(full, last, functools.partial(step, True), running)
        mixed = mixed / total
        turned_ref[pair] = mixed
        lse_ref[pair] = top + jnp.log(total)
        store_rows(out_ref, mixed, first, second)


def attend_grad_kernel(
    order_ref, qnum_ref, knum_ref, q_ref, kv0, kv1, kv2, kv3, grad_ref, turned_ref, lse_ref,
    dq_ref, dkv0, dkv1, dkv2, dkv3, kvs, kvt, total_ref,
):
    sort_keys(knum_ref, (kv0, kv1, kv2, kv3), kvs, kvt)
    total_ref[...] = jnp.zeros_like(total_ref)
    width = 4 * HALF

    @pl.loop(0, q_ref.shape[0] // (2 * HALF))
    def _(pair):
        first, second = order_ref[2 * pair], order_ref[2 * pair + 1]
        low_number, high_number = qnum_ref[first], qnum_ref[second]
        queries = pair_rows(q_ref, first, second, False).astype(bf16)
        grads_f = pair_rows(grad_ref, first, second, True)
        grads = grads_f.astype(bf16)
        both = jnp.concatenate([queries, grads], axis=0)
        positions = pair_positions(low_number, high_number)
        lse = lse_ref[pair]
        dots = jnp.sum(grads_f.T[HEAD_DIM:] * turned_ref[pair], axis=0, keepdims=True)

        def step(masked, counter, query_acc):
            keys = kvs[key_tile(counter), :]
            probs = jnp.exp(score_tile(keys, queries, counter, positions, masked) - lse)
            score_grad = (probs * (product_nt(keys, grads) - dots)).astype(bf16)
            sides = jnp.concatenate([score_grad, probs.astype(bf16)], axis=1)
            total_ref[key_tile(counter), :] += product(sides, both)
            return query_acc + product(kvt[:HEAD_DIM, key_tile(counter)], score_grad)

        full = (low_number * HALF) // TILE
        last = (high_number * HALF) // TILE + 1
        query_acc = lax.fori_loop(0, full, functools.partial(step, False), jnp.zeros((HEAD_DIM, width), f32))
        query_acc = lax.fori_loop(full, last, functools.partial(step, True), query_acc)
        store_rows(dq_ref, query_acc * attn_scale, first, second)

    blocks = dkv0.shape[0] // HALF
    for slot, dkv in enumerate((dkv0, dkv1, dkv2, dkv3)):
        for block in range(blocks):
            dkv[block * HALF : (block + 1) * HALF, :] = total_ref[
                half(knum_ref[slot * blocks + block]), :
            ].astype(bf16)


def expert_kernel(
    expert_ref, me_ref, rows_ref, marked_ref, piece0, piece1, piece2, piece3, router_ref,
    out_ref, in_grad_ref, pre_grad_ref, inner_ref, route_grad_ref, gu_ref, down_ref,
):
    @pl.when(pl.program_id(0) == 0)
    def _():
        part = gu_ref.shape[0] // 4
        for step, piece in enumerate((piece0, piece1, piece2, piece3)):
            place = me_ref[0] ^ step
            gu_ref[pl.ds(pl.multiple_of(place * part, part), part), :] = piece[:part, :]
            down_ref[pl.ds(pl.multiple_of(place * (part // 2), part // 2), part // 2), :] = piece[part:, :]

    rows = rows_ref[...]
    width = rows.shape[1]
    units = down_ref.shape[0]
    pre = product(rows, gu_ref[...])
    gate_pre, up_pre = pre[:, :units], pre[:, units:]
    sigmoid_a = 1.0 / (1.0 + jnp.exp(-gate_pre))
    swish_act = gate_pre * sigmoid_a
    inner_act = (swish_act * up_pre).astype(bf16)
    inner_ref[...] = inner_act
    expert_out = product(inner_act, down_ref[...]).astype(bf16)
    out_ref[...] = expert_out
    uses = marked_ref[:, width : width + EXPERTS].astype(f32)
    probs = gate_of(rows, uses, router_ref[...])
    column = lax.broadcasted_iota(jnp.int32, probs.shape, 1)
    slot_probs = jnp.sum(jnp.where(column == expert_ref[0], probs, 0.0), axis=1, keepdims=True)
    mix_grad = residual_scale * marked_ref[:, :width].astype(f32)
    gate_grad = jnp.sum(mix_grad * expert_out.astype(f32), axis=1, keepdims=True)
    route_grad = (slot_probs * mix_grad).astype(bf16)
    route_grad_ref[...] = route_grad
    inner_grad = product_nt(route_grad, down_ref[...])
    pre_grad_ref[:, :units] = (
        inner_grad * up_pre * sigmoid_a * (1.0 + gate_pre * (1.0 - sigmoid_a))
    ).astype(bf16)
    pre_grad_ref[:, units:] = (inner_grad * swish_act).astype(bf16)
    in_grad_ref[:, :width] = product_nt(pre_grad_ref[...], gu_ref[...]).astype(bf16)
    column = lax.broadcasted_iota(jnp.int32, (rows.shape[0], 128), 1)
    high = gate_grad.astype(bf16).astype(f32)
    in_grad_ref[:, width:] = jnp.where(
        column == expert_ref[0], high, jnp.where(column == EXPERTS + expert_ref[0], gate_grad - high, 0.0)
    ).astype(bf16)


def project_kernel(x_ref, w_ref, gain_ref, cos_ref, sin_ref, normed_ref, q_ref, kv_ref):
    values = x_ref[...].astype(f32)
    normed = (values * inv_rms_of(values) * gain_ref[...]).astype(bf16)
    normed_ref[...] = normed
    projected = product(normed, w_ref[...])
    rotated = projected * cos_ref[...] + turned(projected) * sin_ref[...]
    q_ref[...] = rotated[:, : 2 * HEAD_DIM].astype(bf16) * bf16(attn_scale)
    kv_ref[...] = rotated[:, 2 * HEAD_DIM :].astype(bf16)


def project(rows, head_w, gain, cosine, sine):
    count, width = rows.shape
    tile = 256

    def tiled(columns):
        return pl.BlockSpec((tile, columns), lambda i: (i, 0))

    def whole(array):
        return pl.BlockSpec(array.shape, lambda i: (0, 0))

    columns = (width, 2 * HEAD_DIM, 2 * HEAD_DIM)
    return pl.pallas_call(
        project_kernel,
        grid=(count // tile,),
        out_shape=tuple(jax.ShapeDtypeStruct((count, c), bf16) for c in columns),
        in_specs=[tiled(width), whole(head_w), whole(gain), tiled(4 * HEAD_DIM), tiled(4 * HEAD_DIM)],
        out_specs=tuple(tiled(c) for c in columns),
        compiler_params=pltpu.CompilerParams(vmem_limit_bytes=32 * 1024 * 1024),
        cost_estimate=pl.CostEstimate(flops=600_000_000, bytes_accessed=8_000_000, transcendentals=0),
    )(rows, head_w, gain, cosine, sine)


def call(kernel, outs, operands, flops, held=(), scalars=0, scratch=()):
    count = len(operands)

    def body(*refs):
        kernel(*refs[:count], *refs[count + len(held) :])

    return pl.pallas_call(
        body,
        grid=(1,),
        out_shape=tuple(jax.ShapeDtypeStruct(shape, dtype) for shape, dtype in outs),
        in_specs=[SMEM] * scalars
        + [whole_block(array.shape) for array in operands[scalars:]]
        + [pl.BlockSpec(memory_space=pl.ANY)] * len(held),
        out_specs=tuple(whole_block(shape) for shape, _ in outs),
        scratch_shapes=[pltpu.VMEM(shape, f32) for shape in scratch],
        compiler_params=pltpu.CompilerParams(vmem_limit_bytes=48 * 1024 * 1024),
        cost_estimate=pl.CostEstimate(flops=flops, bytes_accessed=8_000_000, transcendentals=0),
    )(*operands, *held)


def part_of(me_ref, step, part):
    return pl.ds(pl.multiple_of((me_ref[0] ^ step) * part, part), part)


def copies_kernel(x_ref, copies_ref):
    for copy in range(KV_HEADS):
        copies_ref[copy] = x_ref[...]


def shard_kernel(
    head_ref, query_ref, key_ref, value_ref, router_ref, gain1_ref, gain2_ref, out_ref, by_head_ref
):
    rows = query_ref.shape[0]
    lower = lax.broadcasted_iota(jnp.int32, (rows, 128), 1) < HEAD_DIM
    for head in range(KV_HEADS):
        pair = slice(head // 2 * 128, (head // 2 + 1) * 128)
        keys, values = key_ref[:, pair].astype(f32), value_ref[:, pair].astype(f32)
        if head % 2:
            keys = pltpu.roll(keys, HEAD_DIM, 1)
        else:
            values = pltpu.roll(values, HEAD_DIM, 1)
        by_head_ref[:, head * 256 : head * 256 + 128] = query_ref[:, head * 128 : (head + 1) * 128]
        by_head_ref[:, head * 256 + 128 : (head + 1) * 256] = jnp.where(lower, keys, values).astype(bf16)
    out_ref[:rows, :] = by_head_ref[:, pl.ds(pl.multiple_of(head_ref[0] * 256, 256), 256)]
    router = jnp.concatenate([router_ref[...].astype(f32), jnp.zeros((rows, 128 - EXPERTS), f32)], axis=1)
    out_ref[rows : rows + EXPERTS, :] = router.T[:EXPERTS].astype(bf16)
    row = lax.broadcasted_iota(jnp.int32, (16, rows), 0)
    gains = jnp.where(row == 0, gain1_ref[...].astype(f32), jnp.where(row == 1, gain2_ref[...].astype(f32), 0.0))
    out_ref[rows + EXPERTS :, :] = gains.astype(bf16)


def small_kernel(me_ref, piece0, piece1, piece2, piece3, head_w_ref, router_ref, gain1_ref, gain2_ref):
    rows = head_w_ref.shape[0] // 4
    for step, piece in enumerate((piece0, piece1, piece2, piece3)):
        place = part_of(me_ref, step, rows)
        head_w_ref[place, :] = piece[:rows, :]
        router = piece[rows : rows + EXPERTS, :].astype(f32)
        router = jnp.concatenate([router, jnp.zeros((128 - EXPERTS, rows), f32)], axis=0)
        router_ref[place, :] = router.T[:, :EXPERTS].astype(bf16)
        gains = piece[rows + EXPERTS :, :].astype(f32)
        gain1_ref[:, place] = gains[0:1]
        gain2_ref[:, place] = gains[1:2]


def send_kernel(send_ref, rows_ref, out_ref):
    out_ref[...] = product(send_ref[...], rows_ref[...]).astype(bf16)


def middle_kernel(
    me_ref, attn_ref, out0, out1, out2, out3, x_ref, gain_ref, router_ref, uses_ref, send_ref,
    rows_ref, hidden_ref, normed_ref, probs_ref, out_ref,
):
    for head in range(KV_HEADS):
        rows_ref[:, head * 2 * HEAD_DIM : (head + 1) * 2 * HEAD_DIM] = attn_ref[head]
    branch = jnp.zeros(hidden_ref.shape, f32)
    for step, piece in enumerate((out0, out1, out2, out3)):
        branch += product(rows_ref[:, part_of(me_ref, step, piece.shape[0])], piece[...])
    hidden = x_ref[...].astype(f32) + residual_scale * branch
    hidden_ref[...] = hidden
    normed = (hidden * inv_rms_of(hidden) * gain_ref[...]).astype(bf16)
    normed_ref[...] = normed
    out_ref[...] = product(send_ref[...], normed).astype(bf16)
    probs_ref[...] = gate_of(normed, uses_ref[...], router_ref[...])


def token_grad_kernel(
    me_ref, fetch_ref, back_ref, probs_ref, router_ref, hidden_ref, gain_ref, cot_ref, out0, out1, out2, out3,
    hidden_grad_ref, branch_ref, logit_ref, gain_grad_ref, attn_grad_ref,
):
    width = hidden_ref.shape[1]
    fetched = product(fetch_ref[...], back_ref[...])
    gate_grad = fetched[:, width : width + EXPERTS] + fetched[:, width + EXPERTS : width + 2 * EXPERTS]
    probs = probs_ref[...]
    mean_grad = jnp.sum(probs * gate_grad, axis=-1, keepdims=True)
    logit_grad = (probs * (gate_grad - mean_grad)).astype(bf16)
    logit_ref[...] = logit_grad
    normed_grad = fetched[:, :width] + product_nt(logit_grad, router_ref[...])
    hidden = hidden_ref[...]
    hidden_part, gain_grad = norm_back(hidden, inv_rms_of(hidden), gain_ref[...], normed_grad)
    gain_grad_ref[...] = gain_grad
    hidden_grad = cot_ref[...].astype(f32) + hidden_part
    hidden_grad_ref[...] = hidden_grad
    branch = (residual_scale * hidden_grad).astype(bf16)
    branch_ref[...] = branch
    for step, piece in enumerate((out0, out1, out2, out3)):
        attn_grad = product_nt(branch, piece[...]).astype(bf16)
        heads = KV_HEADS // 4
        for head in range(heads):
            columns = slice(head * 2 * HEAD_DIM, (head + 1) * 2 * HEAD_DIM)
            attn_grad_ref[(me_ref[0] ^ step) * heads + head] = attn_grad[:, columns]


def dense_grad_kernel(core_ref, rows_ref, branch_ref, normed_ref, logit_ref, gain_ref, keep_ref, away_ref):
    part, width = keep_ref.shape[1], branch_ref.shape[1]
    logit_grad = logit_ref[...].astype(f32)
    logit_grad = jnp.concatenate(
        [logit_grad, jnp.zeros((logit_grad.shape[0], 128 - EXPERTS), f32)], axis=1
    ).astype(bf16)
    column = lax.broadcasted_iota(jnp.int32, (part, 128), 1)
    for row in range(2):
        for ref, core in ((keep_ref, core_ref[0]), (away_ref, 1 - core_ref[0])):
            columns = pl.ds(pl.multiple_of((2 * row + core) * part, part), part)
            ref[row, :, :width] = product_tn(rows_ref[:, columns], branch_ref[...]).astype(bf16)
            router_grad = product_tn(normed_ref[:, columns], logit_grad)
            gain_grad = jnp.broadcast_to(gain_ref[:, columns], (128, part)).T
            ref[row, :, width:] = jnp.where(column == EXPERTS, gain_grad, router_grad).astype(bf16)


def expert_grad_kernel(core_ref, rows_ref, pre_grad_ref, inner_ref, route_grad_ref, keep_ref, away_ref):
    part = rows_ref.shape[1] // 4
    for row in range(2):
        for ref, core in ((keep_ref, core_ref[0]), (away_ref, 1 - core_ref[0])):
            place = 2 * row + core
            columns = pl.ds(pl.multiple_of(place * part, part), part)
            ref[row, :part, :] = product_tn(rows_ref[:, columns], pre_grad_ref[...]).astype(bf16)
            columns = pl.ds(pl.multiple_of(place * (part // 2), part // 2), part // 2)
            ref[row, part:, :] = product_tn(inner_ref[:, columns], route_grad_ref[...]).astype(bf16)


def dense_split_kernel(place_ref, row_ref, both_ref, other_ref, part0, part1, part2, part3):
    total = (both_ref[row_ref[0]].astype(f32) + other_ref[...].astype(f32)).astype(bf16)
    rows = part0.shape[0]
    for side in range(4):
        for step, ref in enumerate((part0, part1, part2, part3)):

            @pl.when(((place_ref[0] + step) & 3) == side)
            def _():
                ref[...] = total[side * rows : (side + 1) * rows]


def head_grad_kernel(
    dq_ref, dkv0, dkv1, dkv2, dkv3, cos_ref, sin_ref, dense0, dense1, dense2, dense3, out_ref, sent_ref
):
    dkv = dkv0[...].astype(f32) + dkv1[...].astype(f32) + dkv2[...].astype(f32) + dkv3[...].astype(f32)
    for side, grad in enumerate((dq_ref[...], dkv)):
        columns = slice(side * 2 * HEAD_DIM, (side + 1) * 2 * HEAD_DIM)
        out_ref[:, columns] = (grad * cos_ref[:, columns] - turned(grad) * sin_ref[:, columns]).astype(bf16)
    dense = dense0[...].astype(f32) + dense1[...].astype(f32) + dense2[...].astype(f32) + dense3[...].astype(f32)
    tokens = out_ref.shape[0] // KV_HEADS
    empty = jnp.zeros((8, 128), f32)
    for head in range(KV_HEADS):
        sent_ref[head, :tokens, :] = out_ref[head * tokens : (head + 1) * tokens, :]
        mine = dense[head * 8 : (head + 1) * 8]
        lines = [mine[:, side * 256 : (side + 1) * 256] for side in range(4)]
        lines.append(jnp.concatenate([mine[:, 1024:], empty], axis=1))
        lines.append(jnp.concatenate([empty, empty], axis=1))
        sent_ref[head, tokens:, :] = jnp.concatenate(lines, axis=0).astype(bf16)


def head_weight_kernel(core_ref, normed_ref, grads_ref, keep_ref, away_ref):
    part = keep_ref.shape[1]
    for row in range(2):
        for ref, core in ((keep_ref, core_ref[0]), (away_ref, 1 - core_ref[0])):
            columns = pl.ds(pl.multiple_of((2 * row + core) * part, part), part)
            ref[row] = product_tn(normed_ref[:, columns], grads_ref[...]).astype(bf16)


def input_grad_kernel(
    me_ref, grads_ref, w0, w1, w2, w3, x_ref, gain_ref, hidden_grad_ref,
    out_ref, gain0, gain1, gain2, gain3, dense_ref, all_ref,
):
    width = 4 * HEAD_DIM
    tokens = out_ref.shape[0]
    dense = jnp.zeros((grads_ref.shape[1] - tokens, width), f32)
    for head in range(KV_HEADS):
        dense += grads_ref[head, tokens:, :].astype(f32)
    lines = [dense[side * 8 : (side + 1) * 8] for side in range(4)] + [dense[32:40, :128]]
    dense_ref[...] = jnp.concatenate(lines, axis=1).astype(bf16)
    for step, piece in enumerate((w0, w1, w2, w3)):
        part = jnp.zeros((out_ref.shape[0], piece.shape[0]), f32)
        for head in range(KV_HEADS):
            part += product_nt(grads_ref[head, :tokens, :], piece[:, head * width : (head + 1) * width])
        out_ref[:, part_of(me_ref, step, piece.shape[0])] = part
    values = x_ref[...].astype(f32)
    part, gain_grad = norm_back(values, inv_rms_of(values), gain_ref[...], out_ref[...])
    out_ref[...] = hidden_grad_ref[...] + part
    all_ref[...] = gain_grad
    for step, ref in enumerate((gain0, gain1, gain2, gain3)):
        ref[...] = all_ref[:, part_of(me_ref, step, ref.shape[1])]


def gain_block(gain, rows):
    high = gain.astype(bf16).astype(f32)
    return jnp.concatenate([high, gain - high, jnp.zeros((rows - 4, 128), f32)], axis=0)


def line_kernel(part_ref, gain0, gain1, gain2, gain3, dense_ref, out_ref):
    rows, columns = part_ref.shape[0] // 4, part_ref.shape[1]
    for side in range(4):
        out_ref[:rows, side * columns : (side + 1) * columns] = part_ref[side * rows : (side + 1) * rows, :]
    gain = gain0[...] + gain1[...] + gain2[...] + gain3[...]
    gain = jnp.concatenate([gain[:, :128], gain[:, 128:]], axis=0)
    out_ref[:rows, 4 * columns :] = gain_block(gain, rows).astype(bf16)
    dense = dense_ref[...].astype(f32)
    out_ref[rows:, :] = jnp.concatenate([dense, jnp.zeros_like(dense)], axis=0).astype(bf16)


def pack_kernel(place_ref, line0, line1, line2, line3, out_ref, rows_ref):
    rows = line0.shape[0] - 16
    columns = line0.shape[1] - 128
    total = jnp.zeros((rows, columns + 128), f32)
    for step, line in enumerate((line0, line1, line2, line3)):
        total += line[:rows, :].astype(f32)
        place = pl.ds(pl.multiple_of(((place_ref[0] + 4 - step) & 3) * 8, 8), 8)
        rows_ref[place, :] = line[rows:, :].astype(f32)[:8]
    gain = total[0:2, columns:] + total[2:4, columns:]
    weights = total[:, :columns].astype(bf16)
    block = gain_block(gain, rows).astype(bf16)
    dense = rows_ref[...].astype(bf16)
    for head in range(KV_HEADS):
        out_ref[head, :rows, :columns] = weights
        out_ref[head, :rows, columns:] = block
        out_ref[head, rows:, :] = dense


def spread_kernel(
    last_ref, query_ref, key_ref, value_ref, gain_ref, out_grad_ref, router_ref, gain2_ref, column_ref
):
    columns = 4 * HEAD_DIM
    rows = last_ref.shape[1] - 32
    gain_lines = jnp.zeros((rows, 128), f32)
    for head in range(0, KV_HEADS, 2):
        for side in range(4):
            place = slice(side * rows, (side + 1) * rows)
            parts = []
            for step in (0, 1):
                part = last_ref[head + step, :rows, side * columns : (side + 1) * columns].astype(f32)
                query_ref[place, (head + step) * 2 * HEAD_DIM : (head + step + 1) * 2 * HEAD_DIM] = part[:, : 2 * HEAD_DIM]
                parts.append(part)
            pair = slice(head * HEAD_DIM, (head + 2) * HEAD_DIM)
            key_ref[place, pair] = jnp.concatenate([p[:, 2 * HEAD_DIM : 3 * HEAD_DIM] for p in parts], axis=1)
            value_ref[place, pair] = jnp.concatenate([p[:, 3 * HEAD_DIM :] for p in parts], axis=1)
    for head in range(KV_HEADS):
        gain_lines += last_ref[head, :rows, 4 * columns :].astype(f32)
        dense = last_ref[head, rows:, :].astype(f32)
        for place in range(4):
            part = dense[place * 8 : (place + 1) * 8]
            target = slice((place * KV_HEADS + head) * 8, (place * KV_HEADS + head + 1) * 8)
            out_grad_ref[target, :] = part[:, : 4 * columns]
            router_ref[target, :] = part[:, 4 * columns : 4 * columns + EXPERTS]
            column_ref[target, :] = part[:, 4 * columns :]
    gain_ref[:, :128] = gain_lines[0:1] + gain_lines[2:3]
    gain_ref[:, 128:] = gain_lines[1:2] + gain_lines[3:4]
    gain2_ref[...] = column_ref[...].T[EXPERTS : EXPERTS + 1, :]


def gate_of(rows, mask, router_w):
    logits = jnp.where(mask > 0, product(rows, router_w), masked_value)
    exps = jnp.where(mask > 0, jnp.exp(logits - jnp.max(logits, axis=-1, keepdims=True)), 0.0)
    return exps / jnp.maximum(jnp.sum(exps, axis=-1, keepdims=True), 1e-30)


def run_experts(expert, me, rows, marked, pieces, router_w):
    count, width = rows.shape
    part = pieces[0].shape[0] // 3
    units = 4 * part
    tile = 256

    def tiled(columns):
        return pl.BlockSpec((tile, columns), lambda i: (i, 0))

    def whole(array):
        return pl.BlockSpec(array.shape, lambda i: (0, 0))

    columns = (width, width + 128, 2 * units, units, width)
    return pl.pallas_call(
        expert_kernel,
        grid=(count // tile,),
        out_shape=tuple(jax.ShapeDtypeStruct((count, c), bf16) for c in columns),
        in_specs=[SMEM, SMEM, tiled(width), tiled(width + 128)] + [whole(p) for p in pieces] + [whole(router_w)],
        out_specs=tuple(tiled(c) for c in columns),
        scratch_shapes=[pltpu.VMEM((8 * part, 2 * units), bf16), pltpu.VMEM((units, width), bf16)],
        compiler_params=pltpu.CompilerParams(vmem_limit_bytes=56 * 1024 * 1024),
        cost_estimate=pl.CostEstimate(flops=10_000_000_000, bytes_accessed=22_000_000, transcendentals=1_000_000),
    )(expert.astype(jnp.int32).reshape(1), me, rows, marked, *pieces, router_w)


SMEM = pl.BlockSpec(memory_space=pltpu.SMEM)


def whole_block(shape):
    return pl.BlockSpec(tuple(shape), lambda i: (0,) * len(shape))


def attend(numbers, queries, kv_parts):
    rows = queries.shape[0]
    keys = rows * len(kv_parts)
    pairs = rows // (2 * HALF)
    outs = (
        jax.ShapeDtypeStruct((rows, 2 * HEAD_DIM), bf16),
        jax.ShapeDtypeStruct((pairs, HEAD_DIM, 4 * HALF), f32),
        jax.ShapeDtypeStruct((pairs, 1, 4 * HALF), f32),
    )
    return pl.pallas_call(
        attend_kernel,
        grid=(1,),
        out_shape=outs,
        in_specs=[SMEM] * 3 + [whole_block(array.shape) for array in (queries, *kv_parts)],
        out_specs=tuple(whole_block(out.shape) for out in outs),
        scratch_shapes=[pltpu.VMEM((keys, 2 * HEAD_DIM), bf16), pltpu.VMEM((2 * HEAD_DIM, keys), bf16)],
        compiler_params=pltpu.CompilerParams(vmem_limit_bytes=40 * 1024 * 1024),
        cost_estimate=pl.CostEstimate(flops=12_000_000_000, bytes_accessed=4_000_000, transcendentals=5_000_000),
    )(*numbers, queries, *kv_parts)


def attend_grad(numbers, queries, kv_parts, grads, turned, lse):
    rows = queries.shape[0]
    keys = rows * len(kv_parts)
    outs = (jax.ShapeDtypeStruct((rows, 2 * HEAD_DIM), f32),)
    outs += (jax.ShapeDtypeStruct((rows, 2 * HEAD_DIM), bf16),) * 4
    return pl.pallas_call(
        attend_grad_kernel,
        grid=(1,),
        out_shape=outs,
        in_specs=[SMEM] * 3 + [whole_block(array.shape) for array in (queries, *kv_parts, grads, turned, lse)],
        out_specs=tuple(whole_block(out.shape) for out in outs),
        scratch_shapes=[
            pltpu.VMEM((keys, 2 * HEAD_DIM), bf16),
            pltpu.VMEM((2 * HEAD_DIM, keys), bf16),
            pltpu.VMEM((keys, 2 * HEAD_DIM), f32),
        ],
        compiler_params=pltpu.CompilerParams(vmem_limit_bytes=40 * 1024 * 1024),
        cost_estimate=pl.CostEstimate(flops=30_000_000_000, bytes_accessed=6_000_000, transcendentals=5_000_000),
    )(*numbers, queries, *kv_parts, grads, turned, lse)


def block_numbers(block_pairs):
    place = lax.axis_index("x")
    groups = block_pairs.reshape(4, 8)
    groups = groups[(place - jnp.arange(4)) & 3]
    numbers = jnp.stack([groups, 63 - groups], axis=-1).reshape(-1)
    own = numbers[:16]
    rank = jnp.sum((own[None, :] < own[:, None]).astype(jnp.int32), axis=1)
    spots = jnp.arange(16, dtype=jnp.int32)
    order = jnp.sum(jnp.where(rank[None, :] == spots[:, None], spots[None, :], 0), axis=1)
    return (order, own, numbers)


def on_device(
    block_input,
    routes,
    block_pairs,
    norm1_gain,
    w_query,
    w_key,
    w_value,
    w_out,
    norm2_gain,
    w_router,
    w_gate,
    w_up,
    w_down,
    cotangent,
):
    tokens, width = block_input.shape[1:]
    head = lax.axis_index(ZY)
    expert = lax.axis_index(CTX)
    shard_rows = w_query.shape[0]
    own_input = block_input[0]

    core = lax.axis_index("core").astype(jnp.int32).reshape(1)
    place = lax.axis_index("x").astype(jnp.int32).reshape(1)
    me = lax.axis_index(("yl", "core")).astype(jnp.int32).reshape(1)
    small_shard, by_head = call(
        shard_kernel,
        [((shard_rows + EXPERTS + 16, 4 * HEAD_DIM), bf16), ((shard_rows, KV_HEADS * 4 * HEAD_DIM), bf16)],
        (
            head.astype(jnp.int32).reshape(1), w_query, w_key, w_value, w_router,
            norm1_gain.reshape(1, -1), norm2_gain.reshape(1, -1),
        ),
        1_000_000,
        scalars=1,
    )
    small_pieces = pieces_direct(small_shard)
    (copies,) = call(copies_kernel, [((KV_HEADS, tokens, width), bf16)], (own_input,), 1_000_000)
    group_input = exchange(copies.reshape(-1, width), ZY)
    head_w, router_w, gain_one, gain_two = call(
        small_kernel,
        [((width, 4 * HEAD_DIM), bf16), ((width, EXPERTS), bf16), ((1, width), f32), ((1, width), f32)],
        (me, *small_pieces),
        1_000_000,
        scalars=1,
    )

    numbers = block_numbers(block_pairs)
    group_pos = (numbers[1][:, None] * HALF + jnp.arange(HALF, dtype=jnp.int32)[None, :]).reshape(-1)
    cosine, sine = rope_tables(group_pos)

    chosen = routes[0]
    uses = jnp.sum(
        (chosen[:, :, None] == jnp.arange(EXPERTS, dtype=jnp.int32)[None, None, :]).astype(f32), axis=1
    )
    earlier = jnp.tril(jnp.ones((tokens, tokens), bf16), -1)
    rank = product(earlier, uses.astype(bf16)).astype(jnp.int32)
    rank = jnp.where(uses > 0, rank, -1)
    slot = jnp.arange(CAP, dtype=jnp.int32)
    send = (rank.T[:, None, :] == slot[None, :, None]).astype(bf16).reshape(EXPERTS * CAP, tokens)
    fetch = (rank[:, :, None] == slot[None, None, :]).astype(bf16).reshape(tokens, EXPERTS * CAP)

    group_normed, queries, kv_own = project(group_input, head_w, gain_one, cosine, sine)
    kv_parts = [kv_own] + [turn(kv_own, "x", step) for step in (1, 2, 3)]

    out_other = swap(w_out, "yl")
    expert_shard = jnp.concatenate([jnp.concatenate([w_gate[0], w_up[0]], axis=1), w_down[0]], axis=0)
    expert_other = swap(expert_shard, "yl")
    marked = jnp.concatenate(
        [cotangent[0], uses.astype(bf16), jnp.zeros((tokens, 128 - EXPERTS), bf16)], axis=1
    )
    (marked_sent,) = call(
        send_kernel,
        [((EXPERTS * CAP, width + 128), bf16)],
        (send, marked),
        500_000_000,
        held=(*kv_parts[1:], out_other, expert_other),
    )
    marked_arrived = exchange(marked_sent, CTX)

    attn_group, attn_turned, lse = attend(numbers, queries, kv_parts)

    out_pieces = pieces_by_row(w_out, out_other)

    attn_back = exchange(tie(attn_group, marked_arrived), ZY)
    expert_pieces = pieces_by_row(expert_shard, expert_other)
    attn_rows, hidden, normed2, gate_probs, outgoing = call(
        middle_kernel,
        [
            ((tokens, HEADS * HEAD_DIM), bf16),
            ((tokens, width), f32),
            ((tokens, width), bf16),
            ((tokens, EXPERTS), f32),
            ((EXPERTS * CAP, width), bf16),
        ],
        (
            me, attn_back.reshape(KV_HEADS, tokens, 2 * HEAD_DIM), *out_pieces, own_input, gain_two, router_w,
            uses, send,
        ),
        800_000_000,
        held=expert_pieces,
        scalars=1,
    )
    arrived = exchange(outgoing, CTX)

    expert_out, in_grad, pre_grad, inner_act, route_grad = run_experts(
        expert, me, arrived, marked_arrived, expert_pieces, router_w
    )
    back = exchange(in_grad, CTX)
    by_head_sent = tie(by_head, normed2)
    head_pieces = pieces_by_row(by_head_sent, swap(by_head_sent, "yl"))
    expert_shape = ((2, *expert_shard.shape), bf16)
    expert_both = join_core(
        *call(
            expert_grad_kernel,
            [expert_shape, expert_shape],
            (core, arrived, pre_grad, inner_act, route_grad),
            5_000_000_000,
            held=(head_pieces[2],),
            scalars=1,
        )
    )

    hidden_grad, branch_grad, logit_grad, gain_two_grad, attn_grad = call(
        token_grad_kernel,
        [
            ((tokens, width), f32),
            ((tokens, width), bf16),
            ((tokens, EXPERTS), bf16),
            ((1, width), f32),
            ((KV_HEADS, tokens, 2 * HEAD_DIM), bf16),
        ],
        (me, fetch, back, gate_probs, router_w, hidden, gain_two, cotangent[0], *out_pieces),
        800_000_000,
        held=(expert_both, *head_pieces),
        scalars=1,
    )

    group_grad = exchange(attn_grad.reshape(KV_HEADS * tokens, 2 * HEAD_DIM), ZY)
    dq, *dkv_parts = attend_grad(numbers, queries, kv_parts, group_grad, attn_turned, lse)
    dkv_turned = [turn(dkv_parts[step], "x", -step) for step in (1, 2, 3)]
    dense_shape = ((2, shard_rows, width + 128), bf16)
    dense_both = join_core(
        *call(
            dense_grad_kernel,
            [dense_shape, dense_shape],
            (core, attn_rows, branch_grad, normed2, logit_grad, gain_two_grad),
            400_000_000,
            scalars=1,
        )
    )
    row = lax.axis_index("yl").astype(jnp.int32).reshape(1)
    dense_other = swap(lax.dynamic_index_in_dim(dense_both, 1 - row[0], 0, keepdims=False), "yl")
    dense_parts = call(
        dense_split_kernel,
        [((shard_rows // 4, width + 128), bf16)] * 4,
        (place, row, dense_both, dense_other),
        1_000_000,
        held=(dq,),
        scalars=2,
    )
    dense_turned = [turn(dense_parts[step], "x", step) for step in (1, 2, 3)]

    grads, grads_sent = call(
        head_grad_kernel,
        [((KV_HEADS * tokens, 4 * HEAD_DIM), bf16), ((KV_HEADS, tokens + 48, 4 * HEAD_DIM), bf16)],
        (dq, dkv_parts[0], *dkv_turned, cosine, sine, dense_parts[0], *dense_turned),
        100_000_000,
    )
    token_grads = exchange(grads_sent.reshape(-1, 4 * HEAD_DIM), ZY)
    head_shape = ((2, shard_rows, 4 * HEAD_DIM), bf16)
    head_both = join_core(
        *call(head_weight_kernel, [head_shape, head_shape], (core, group_normed, grads), 600_000_000, scalars=1)
    )
    head_part = scatter_row(head_both).astype(bf16)

    returned = exchange(tie(expert_out, token_grads, head_part), CTX)


    gain_shape = ((1, shard_rows), f32)
    input_grad, *gain_parts, dense = call(
        input_grad_kernel,
        [((tokens, width), f32)] + [gain_shape] * 4 + [((8, width + 128), bf16)],
        (
            me, token_grads.reshape(grads_sent.shape), *head_pieces, own_input, gain_one, hidden_grad,
        ),
        600_000_000,
        scalars=1,
        scratch=[(1, width)],
    )
    later = (gain_parts[0][0, 0] * 0.0).astype(jnp.int32)
    expert_away = lax.dynamic_slice_in_dim(expert_both, 1 - row[0] + later, 1, 0)[0]
    expert_other = swap(expert_away, "yl")
    expert_sums = lax.dynamic_index_in_dim(expert_both, row[0], 0, keepdims=False).astype(f32)
    expert_sums = expert_sums + expert_other.astype(f32)
    gain_turned = [
        lax.ppermute(gain_parts[step], ("yl", "core"), [(i, i ^ step) for i in range(4)]) for step in (1, 2, 3)
    ]
    (line,) = call(
        line_kernel,
        [((shard_rows // 4 + 16, width + 128), bf16)],
        (head_part, gain_parts[0], *gain_turned, dense),
        1_000_000,
    )
    (last,) = call(
        pack_kernel,
        [((KV_HEADS, shard_rows // 4 + 32, width + 128), bf16)],
        (place, *all_x(line)),
        1_000_000,
        held=(returned, expert_other),
        scalars=1,
        scratch=[(32, width + 128)],
    )
    last = exchange(last.reshape(-1, width + 128), ZY).reshape(last.shape)
    grad_query, grad_key, grad_value, gain_one_grad, grad_out, grad_router, gain_two_grad = call(
        spread_kernel,
        [
            ((shard_rows, HEADS * HEAD_DIM), f32),
            ((shard_rows, KV_HEADS * HEAD_DIM), f32),
            ((shard_rows, KV_HEADS * HEAD_DIM), f32),
            gain_shape,
            ((shard_rows, width), f32),
            ((shard_rows, EXPERTS), f32),
            gain_shape,
        ],
        (last,),
        1_000_000,
        scratch=[(shard_rows, 128)],
    )

    spread = gate_probs[:, :, None] * fetch.astype(f32).reshape(tokens, EXPERTS, CAP)
    weights = spread.reshape(tokens, EXPERTS * CAP)
    weights_hi = weights.astype(bf16)
    weights_lo = (weights - weights_hi.astype(f32)).astype(bf16)
    mixture = product(weights_hi, returned) + product(weights_lo, returned)
    output = hidden + residual_scale * mixture

    return (
        output.astype(bf16)[None],
        input_grad[None],
        gain_one_grad.reshape(-1),
        grad_query,
        grad_key,
        grad_value,
        grad_out,
        gain_two_grad.reshape(-1),
        grad_router,
        expert_sums[None, :shard_rows, : width // 2],
        expert_sums[None, :shard_rows, width // 2 :],
        expert_sums[None, shard_rows:],
    )


def solution(mesh):
    fine = Mesh(mesh.devices.reshape(4, 4, 2, 2, 2), EVERY)
    rows, shards = P(("yl", "core"), CTX, None), P(("yl", "core"), None)
    gain, experts = P(("yl", "core")), P(CTX, ("yl", "core"), None)
    return jax.shard_map(
        on_device,
        mesh=fine,
        in_specs=(
            rows, rows, P(), gain, shards, shards, shards, shards, gain, shards, experts, experts, experts, rows,
        ),
        out_specs=(
            rows, rows, gain, shards, shards, shards, shards, gain, shards, experts, experts, experts,
        ),
        check_vma=False,
    )
```

profile of v0, /device:TPU:2, one launch (start us, length us, event | category | flops | bytes accessed | tf_op | source)
XLA Modules:
  0.0 488.0 jit_solution(3492936335287991856)
XLA Ops:
  1.6 1.5 shard_map.229
  3.1 8.1 %all-to-all-start = ((bf16[8,128,1024]{2,1,0:T(8,128)(2,1)}), bf16[8,128,1024]{2,1,0:T(8,128)(2,1)}, u32[]{:S(2)}, u32[]{:S(2)}) async-start(bf16[8,128,1024]{2,1,0:T(8,128)(2,1)} %shard_map.229), calls=%async_computation | async-start | bytes 4194304 | tf_op jit(solution)/shard_map/all_to_all | solution.py:58
  16.3 1.3 collective-permute-start.6
  19.0 3.0 multiply_sine_fusion
  22.1 3.3 concatenate.22.cos_ref.refs_5_
  26.1 3.8 concatenate.24.sin_ref.refs_6_
  30.0 9.6 %collective-permute-done.1.refs_3_ = bf16[304,256]{1,0:T(8,128)(2,1)S(1)} collective-permute-done((bf16[304,256]{1,0:T(8,128)(2,1)S(1)}, bf16[304,256]{1,0:T(8,128)(2,1)S(1)}, u32[]{:S(2)}, u32[]{:S(2)}) %collective-permute-start.1) | collective-permute-done | bytes 155680 | tf_op jit(solution)/shard_map/ppermute | solution.py:71
  40.2 1.7 collective-permute-done.2.refs_4_
  45.3 4.5 shard_map.232
  49.8 1.4 copy-done.4
  51.9 1.5 collective-permute-start.3
  54.5 2.2 collective-permute-start.5
  59.0 10.8 %collective-permute-done.6.refs_5_.refs_4_.refs_10_ = bf16[256,1024]{1,0:T(8,128)(2,1)S(1)} collective-permute-done((bf16[256,1024]{1,0:T(8,128)(2,1)}, bf16[256,1024]{1,0:T(8,128)(2,1)S(1)}, u32[]{:S(2)}, u32[]{:S(2)}) %collective-permute-start.6) | collective-permute-done | bytes 524320 | tf_op jit(solution)/shard_map/ppermute | solution.py:46
  69.9 2.9 shard_map.234
  72.8 11.3 %all-to-all-start.1 = ((bf16[32,48,1152]{2,1,0:T(8,128)(2,1)}), bf16[32,48,1152]{2,1,0:T(8,128)(2,1)}, u32[]{:S(2)}, u32[]{:S(2)}) async-start(bf16[32,48,1152]{2,1,0:T(8,128)(2,1)} %bitcast.92), calls=%async_computation.1 | async-start | bytes 7077888 | tf_op jit(solution)/shard_map/all_to_all | solution.py:58
  86.8 23.3 %shard_map.233 = (bf16[1024,128]{1,0:T(8,128)(2,1)S(1)}, f32[8,64,256]{2,1,0:T(8,128)S(1)}, f32[8,1,256]{2,1,0:T(1,128)S(1)}) custom-call(s32[16]{0:T(128)S(1)} %select_reduce_fusion.order_ref, s32[16]{0:T(128)S(1)} %lt.40.qnum_ref, s32[64]{0:T(128)S(1)} %reshape.205.knum_ref, bf16[1024,128]{1,0:T(8,128)(2,1)S(1)} %copy-done.32, ...), custom_call_target="tpu_custom_call" | custom-call | flops 12000000000 | bytes 4000000 | tf_op jit(solution)/shard_map/pallas_call | solution.py:656
  112.2 16.4 %all-to-all-done.1 = bf16[32,48,1152]{2,1,0:T(8,128)(2,1)} async-done(((bf16[32,48,1152]{2,1,0:T(8,128)(2,1)}), bf16[32,48,1152]{2,1,0:T(8,128)(2,1)}, u32[]{:S(2)}, u32[]{:S(2)}) %all-to-all-start.1) | async-done | bytes 3538976 | tf_op jit(solution)/shard_map/all_to_all | solution.py:58
  131.7 6.6 %all-to-all-start.2 = ((bf16[8,128,128]{2,1,0:T(8,128)(2,1)}), bf16[8,128,128]{2,1,0:T(8,128)(2,1)}, u32[]{:S(2)}, u32[]{:S(2)}) async-start(bf16[8,128,128]{2,1,0:T(8,128)(2,1)} %bitcast.91), calls=%async_computation.2 | async-start | bytes 524288 | tf_op jit(solution)/shard_map/all_to_all | solution.py:58
  138.3 8.9 %all-to-all-done.2.refs_1_ = bf16[8,128,128]{2,1,0:T(8,128)(2,1)} async-done(((bf16[8,128,128]{2,1,0:T(8,128)(2,1)}), bf16[8,128,128]{2,1,0:T(8,128)(2,1)}, u32[]{:S(2)}, u32[]{:S(2)}) %all-to-all-start.2) | async-done | bytes 262176 | tf_op jit(solution)/shard_map/all_to_all | solution.py:58
  148.0 4.7 shard_map.235
  155.5 5.6 %all-to-all-start.3 = ((bf16[32,48,1024]{2,1,0:T(8,128)(2,1)}), bf16[32,48,1024]{2,1,0:T(8,128)(2,1)}, u32[]{:S(2)}, u32[]{:S(2)}) async-start(bf16[32,48,1024]{2,1,0:T(8,128)(2,1)} %bitcast.95), calls=%async_computation.3 | async-start | bytes 6291456 | tf_op jit(solution)/shard_map/all_to_all | solution.py:58
  165.5 34.9 %all-to-all-done.3 = bf16[32,48,1024]{2,1,0:T(8,128)(2,1)} async-done(((bf16[32,48,1024]{2,1,0:T(8,128)(2,1)}), bf16[32,48,1024]{2,1,0:T(8,128)(2,1)}, u32[]{:S(2)}, u32[]{:S(2)}) %all-to-all-start.3) | async-done | bytes 3145760 | tf_op jit(solution)/shard_map/all_to_all | solution.py:58
  200.4 19.1 %shard_map.236 = (bf16[1536,1024]{1,0:T(8,128)(2,1)}, bf16[1536,1152]{1,0:T(8,128)(2,1)}, bf16[1536,1024]{1,0:T(8,128)(2,1)}, bf16[1536,512]{1,0:T(8,128)(2,1)}, bf16[1536,1024]{1,0:T(8,128)(2,1)}) custom-call(s32[1]{0:T(128)} %bitcast.23.expert_ref, s32[1]{0:T(128)} %bitcast.refs_0_.me_ref, bf16[1536,1024]{1,0:T(8,128)(2,1)} %bitcast.25.rows_ref.refs_1_, ...), custom_call_target="tpu_custom_call" | custom-call | flops 10000000000 | bytes 22000000 | tf_op jit(solution)/shard_map/pallas_call | solution.py:628
  219.5 9.4 %all-to-all-start.4 = ((bf16[32,48,1152]{2,1,0:T(8,128)(2,1)}), bf16[32,48,1152]{2,1,0:T(8,128)(2,1)}, u32[]{:S(2)}, u32[]{:S(2)}) async-start(bf16[32,48,1152]{2,1,0:T(8,128)(2,1)} %bitcast.93), calls=%async_computation.4 | async-start | bytes 7077888 | tf_op jit(solution)/shard_map/all_to_all | solution.py:58
  228.9 1.4 copy-done.40
  230.3 10.1 %shard_map.237 = (bf16[2,384,1024]{2,1,0:T(8,128)(2,1)S(1)}, bf16[2,384,1024]{2,1,0:T(8,128)(2,1)}) custom-call(s32[1]{0:T(128)} %bitcast.28.refs_0_, bf16[1536,1024]{1,0:T(8,128)(2,1)} %bitcast.25.rows_ref.refs_1_, bf16[1536,1024]{1,0:T(8,128)(2,1)} %get-tuple-element.82.refs_2_, bf16[1536,512]{1,0:T(8,128)(2,1)S(1)} %copy-done.40, ...), custom_call_target="tpu_custom_call" | custom-call | flops 5000000000 | bytes 8000000 | tf_op jit(solution)/shard_map/pallas_call | solution.py:349
  243.2 2.3 copy.60
  246.8 3.9 add_convert_fusion.refs_12_
  250.7 23.7 %all-to-all-done.4 = bf16[32,48,1152]{2,1,0:T(8,128)(2,1)} async-done(((bf16[32,48,1152]{2,1,0:T(8,128)(2,1)}), bf16[32,48,1152]{2,1,0:T(8,128)(2,1)}, u32[]{:S(2)}, u32[]{:S(2)}) %all-to-all-start.4) | async-done | bytes 3538976 | tf_op jit(solution)/shard_map/all_to_all | solution.py:58
  277.3 4.5 shard_map.238
  283.7 6.0 %all-to-all-start.5 = ((bf16[8,128,128]{2,1,0:T(8,128)(2,1)}), bf16[8,128,128]{2,1,0:T(8,128)(2,1)}, u32[]{:S(2)}, u32[]{:S(2)}) async-start(bf16[8,128,128]{2,1,0:T(8,128)(2,1)} %copy-done.24), calls=%async_computation.5 | async-start | bytes 524288 | tf_op jit(solution)/shard_map/all_to_all | solution.py:58
  289.7 1.9 add_convert_fusion.1.refs_2_
  292.5 2.3 collective-permute-start.20
  294.8 4.4 all-to-all-done.5
  301.9 21.9 %shard_map.239 = (f32[1024,128]{1,0:T(8,128)S(1)}, bf16[1024,128]{1,0:T(8,128)(2,1)S(1)}, bf16[1024,128]{1,0:T(8,128)(2,1)S(1)}, bf16[1024,128]{1,0:T(8,128)(2,1)S(1)}, bf16[1024,128]{1,0:T(8,128)(2,1)S(1)}) custom-call(s32[16]{0:T(128)S(1)} %copy-done.39, s32[16]{0:T(128)S(1)} %lt.40.qnum_ref, s32[64]{0:T(128)S(1)} %reshape.205.knum_ref, ...), custom_call_target="tpu_custom_call" | custom-call | flops 30000001024 | bytes 6000000 | tf_op jit(solution)/shard_map/pallas_call | solution.py:673
  323.8 3.2 collective-permute-start.16
  327.1 1.6 collective-permute-start.18
  328.6 1.4 shard_map.241
  330.1 2.6 collective-permute-start.21
  333.8 2.5 collective-permute-start.23
  336.3 3.2 collective-permute-done.17.refs_3_
  339.5 1.4 collective-permute-done.18.refs_4_
  340.9 2.8 collective-permute-done.21.refs_8_
  344.2 1.7 shard_map.242
  346.8 3.8 all-to-all-start.6
  350.7 2.2 collective-permute-start.25
  352.9 11.8 %collective-permute-done.25 = bf16[256,256]{1,0:T(8,128)(2,1)S(1)} collective-permute-done((bf16[256,256]{1,0:T(8,128)(2,1)S(1)}, bf16[256,256]{1,0:T(8,128)(2,1)S(1)}, u32[]{:S(2)}, u32[]{:S(2)}) %collective-permute-start.25) | collective-permute-done | bytes 131104 | tf_op jit(solution)/shard_map/ppermute | solution.py:46
  368.8 15.2 %all-to-all-start.7 = ((bf16[32,48,1024]{2,1,0:T(8,128)(2,1)}), bf16[32,48,1024]{2,1,0:T(8,128)(2,1)}, u32[]{:S(2)}, u32[]{:S(2)}) async-start(bf16[32,48,1024]{2,1,0:T(8,128)(2,1)} %bitcast.94), calls=%async_computation.7 | async-start | bytes 6291456 | tf_op jit(solution)/shard_map/all_to_all | solution.py:58
  384.0 4.8 shard_map.244
  390.3 1.9 collective-permute-start.27
  392.3 47.1 %collective-permute-done.27.refs_3_ = f32[1,256]{1,0:T(1,128)S(1)} collective-permute-done((f32[1,256]{1,0:T(1,128)S(1)}, f32[1,256]{1,0:T(1,128)S(1)}, u32[]{:S(2)}, u32[]{:S(2)}) %collective-permute-start.27) | collective-permute-done | bytes 1056 | tf_op jit(solution)/shard_map/ppermute | solution.py:896
  439.6 1.6 collective-permute-start.30
  441.2 2.5 collective-permute-start.31
  443.7 3.4 collective-permute-done.29.refs_2_
  447.1 1.6 collective-permute-done.30.refs_3_
  448.7 2.7 collective-permute-done.31.refs_4_
  451.4 1.5 shard_map.246
  452.9 7.0 %all-to-all-start.8 = ((bf16[8,96,1152]{2,1,0:T(8,128)(2,1)}), bf16[8,96,1152]{2,1,0:T(8,128)(2,1)S(1)}, u32[]{:S(2)}, u32[]{:S(2)}) async-start(bf16[8,96,1152]{2,1,0:T(8,128)(2,1)} %shard_map.246), calls=%async_computation.8 | async-start | bytes 3538944 | tf_op jit(solution)/shard_map/all_to_all | solution.py:58
  460.9 1.4 copy.61
  462.3 1.4 convert_add_fusion
  465.6 2.5 fusion.7
  468.2 3.3 fusion.3
  471.4 13.6 %all-to-all-done.8.refs_0_ = bf16[8,96,1152]{2,1,0:T(8,128)(2,1)S(1)} async-done(((bf16[8,96,1152]{2,1,0:T(8,128)(2,1)}), bf16[8,96,1152]{2,1,0:T(8,128)(2,1)S(1)}, u32[]{:S(2)}, u32[]{:S(2)}) %all-to-all-start.8) | async-done | bytes 1769504 | tf_op jit(solution)/shard_map/all_to_all | solution.py:58
  485.0 1.8 shard_map.247
  (222 shorter events, 53.1 us)
Async XLA Ops:
  3.1 8.2 %copy-start.55 = (bf16[256,32]{0,1:T(8,128)(2,1)S(1)}, bf16[256,32]{0,1:T(8,128)(2,1)}, u32[]{:S(2)}) copy-start(bf16[256,32]{0,1:T(8,128)(2,1)} %param.23) | copy-start | bytes 49156
  3.1 8.3 %copy-start.58 = (bf16[256]{0:T(256)(128)(2,1)S(1)}, bf16[256]{0:T(256)(128)(2,1)}, u32[]{:S(2)}) copy-start(bf16[256]{0:T(256)(128)(2,1)} %param.17) | copy-start | bytes 1540
  3.1 8.3 %copy-start.59 = (bf16[256]{0:T(256)(128)(2,1)S(1)}, bf16[256]{0:T(256)(128)(2,1)}, u32[]{:S(2)}) copy-start(bf16[256]{0:T(256)(128)(2,1)} %param.22) | copy-start | bytes 1540
  3.1 8.3 %copy-start.19 = (bf16[256,1024]{1,0:T(8,128)(2,1)S(1)}, bf16[256,1024]{1,0:T(8,128)(2,1)}, u32[]{:S(2)}) copy-start(bf16[256,1024]{1,0:T(8,128)(2,1)} %refs_1_.1) | copy-start | bytes 1572868
  3.1 8.4 %copy-start.25 = (bf16[256,512]{1,0:T(8,128)(2,1)S(1)}, bf16[256,512]{1,0:T(8,128)(2,1)}, u32[]{:S(2)}) copy-start(bf16[256,512]{1,0:T(8,128)(2,1)} %refs_2_.2) | copy-start | bytes 786436
  3.1 8.3 %copy-start.26 = (bf16[256,512]{1,0:T(8,128)(2,1)S(1)}, bf16[256,512]{1,0:T(8,128)(2,1)}, u32[]{:S(2)}) copy-start(bf16[256,512]{1,0:T(8,128)(2,1)} %refs_3_.1) | copy-start | bytes 786436
  3.1 11.5 %copy-start.46 = (bf16[1,128,1024]{2,1,0:T(8,128)(2,1)S(1)}, bf16[1,128,1024]{2,1,0:T(8,128)(2,1)}, u32[]{:S(2)}) copy-start(bf16[1,128,1024]{2,1,0:T(8,128)(2,1)} %param.26) | copy-start | bytes 786436
  3.1 11.5 %copy-start.47 = (bf16[1,256,512]{2,1,0:T(8,128)(2,1)S(1)}, bf16[1,256,512]{2,1,0:T(8,128)(2,1)}, u32[]{:S(2)}) copy-start(bf16[1,256,512]{2,1,0:T(8,128)(2,1)} %param.25) | copy-start | bytes 786436
  3.1 11.5 %copy-start.48 = (bf16[1,256,512]{2,1,0:T(8,128)(2,1)S(1)}, bf16[1,256,512]{2,1,0:T(8,128)(2,1)}, u32[]{:S(2)}) copy-start(bf16[1,256,512]{2,1,0:T(8,128)(2,1)} %param.24) | copy-start | bytes 786436
  3.1 42.2 %all-to-all-start = ((bf16[8,128,1024]{2,1,0:T(8,128)(2,1)}), bf16[8,128,1024]{2,1,0:T(8,128)(2,1)}, u32[]{:S(2)}, u32[]{:S(2)}) async-start(bf16[8,128,1024]{2,1,0:T(8,128)(2,1)} %shard_map.229), calls=%async_computation | async-start | bytes 4194304 | tf_op jit(solution)/shard_map/all_to_all | solution.py:58
  11.2 6.4 %copy-start.57 = (s32[32]{0:T(128)S(1)}, s32[32]{0:T(128)}, u32[]{:S(2)}) copy-start(s32[32]{0:T(128)} %param.16) | copy-start | bytes 388
  12.7 17.2 %collective-permute-start = (bf16[304,256]{1,0:T(8,128)(2,1)S(1)}, bf16[304,256]{1,0:T(8,128)(2,1)S(1)}, u32[]{:S(2)}, u32[]{:S(2)}) collective-permute-start(bf16[304,256]{1,0:T(8,128)(2,1)S(1)} %get-tuple-element.69.refs_1_), channel_id=1, source_target_pairs={{0,1},{1,0},{2,3},{3,2},{4,5},{5,4},{6,7},{7,6},{8,9},{9,8},{10,11... | collective-permute-start | bytes 466952 | tf_op jit(solution)/shard_map/ppermute | solution.py:71
  12.7 26.8 %collective-permute-start.1 = (bf16[304,256]{1,0:T(8,128)(2,1)S(1)}, bf16[304,256]{1,0:T(8,128)(2,1)S(1)}, u32[]{:S(2)}, u32[]{:S(2)}) collective-permute-start(bf16[304,256]{1,0:T(8,128)(2,1)S(1)} %get-tuple-element.69.refs_1_), channel_id=1, source_target_pairs={{0,2},{1,3},{2,0},{3,1},{4,6},{5,7},{6,4},{7,5},{8,10},{9,11},{10,... | collective-permute-start | bytes 466952 | tf_op jit(solution)/shard_map/ppermute | solution.py:71
  13.4 28.5 %collective-permute-start.2 = (bf16[304,256]{1,0:T(8,128)(2,1)S(1)}, bf16[304,256]{1,0:T(8,128)(2,1)S(1)}, u32[]{:S(2)}, u32[]{:S(2)}) collective-permute-start(bf16[304,256]{1,0:T(8,128)(2,1)S(1)} %get-tuple-element.69.refs_1_), channel_id=1, source_target_pairs={{0,3},{1,2},{2,1},{3,0},{4,7},{5,6},{6,5},{7,4},{8,11},{9,10},{10,... | collective-permute-start | bytes 466952 | tf_op jit(solution)/shard_map/ppermute | solution.py:71
  15.6 54.3 %collective-permute-start.7 = (bf16[384,1024]{1,0:T(8,128)(2,1)}, bf16[384,1024]{1,0:T(8,128)(2,1)}, u32[]{:S(2)}, u32[]{:S(2)}) collective-permute-start(bf16[384,1024]{1,0:T(8,128)(2,1)} %pad_maximum_fusion.refs_11_.piece0), channel_id=1, source_target_pairs={{0,2},{2,0},{1,3},{3,1},{4,6},{6,4},{5,7},{7,5},{8,10},{10,8},{9,1... | collective-permute-start | bytes 2359304 | tf_op jit(solution)/shard_map/ppermute | solution.py:46
  16.3 53.6 %collective-permute-start.6 = (bf16[256,1024]{1,0:T(8,128)(2,1)}, bf16[256,1024]{1,0:T(8,128)(2,1)S(1)}, u32[]{:S(2)}, u32[]{:S(2)}) collective-permute-start(bf16[256,1024]{1,0:T(8,128)(2,1)} %refs_8_.1), channel_id=1, source_target_pairs={{0,2},{2,0},{1,3},{3,1},{4,6},{6,4},{5,7},{7,5},{8,10},{10,8},{9,1... | collective-permute-start | bytes 1572872 | tf_op jit(solution)/shard_map/ppermute | solution.py:46
  51.9 18.0 %collective-permute-start.3 = (bf16[1024,128]{1,0:T(8,128)(2,1)}, bf16[1024,128]{1,0:T(8,128)(2,1)}, u32[]{:S(2)}, u32[]{:S(2)}) collective-permute-start(bf16[1024,128]{1,0:T(8,128)(2,1)} %get-tuple-element.73.kv0), channel_id=1, source_target_pairs={{0,32},{32,64},{64,96},{96,0},{1,33},{33,65},{65,97},{97,1},{2,34}... | collective-permute-start | bytes 786440 | tf_op jit(solution)/shard_map/ppermute | solution.py:50
  53.4 16.5 %collective-permute-start.4 = (bf16[1024,128]{1,0:T(8,128)(2,1)}, bf16[1024,128]{1,0:T(8,128)(2,1)}, u32[]{:S(2)}, u32[]{:S(2)}) collective-permute-start(bf16[1024,128]{1,0:T(8,128)(2,1)} %get-tuple-element.73.kv0), channel_id=1, source_target_pairs={{0,64},{32,96},{64,0},{96,32},{1,65},{33,97},{65,1},{97,33},{2,66}... | collective-permute-start | bytes 786440 | tf_op jit(solution)/shard_map/ppermute | solution.py:50
  54.5 15.4 %collective-permute-start.5 = (bf16[1024,128]{1,0:T(8,128)(2,1)}, bf16[1024,128]{1,0:T(8,128)(2,1)}, u32[]{:S(2)}, u32[]{:S(2)}) collective-permute-start(bf16[1024,128]{1,0:T(8,128)(2,1)} %get-tuple-element.73.kv0), channel_id=1, source_target_pairs={{0,96},{32,0},{64,32},{96,64},{1,97},{33,1},{65,33},{97,65},{2,98}... | collective-permute-start | bytes 786440 | tf_op jit(solution)/shard_map/ppermute | solution.py:50
  72.8 11.9 %copy-start.54 = (s32[4,8,1]{1,0,2:T(4,128)S(1)}, s32[4,8,1]{1,0,2:T(4,128)}, u32[]{:S(2)}) copy-start(s32[4,8,1]{1,0,2:T(4,128)} %copy-done.53) | copy-start | bytes 388
  72.8 55.7 %all-to-all-start.1 = ((bf16[32,48,1152]{2,1,0:T(8,128)(2,1)}), bf16[32,48,1152]{2,1,0:T(8,128)(2,1)}, u32[]{:S(2)}, u32[]{:S(2)}) async-start(bf16[32,48,1152]{2,1,0:T(8,128)(2,1)} %bitcast.92), calls=%async_computation.1 | async-start | bytes 7077888 | tf_op jit(solution)/shard_map/all_to_all | solution.py:58
  84.1 54.1 %collective-permute-start.10 = (bf16[384,1024]{1,0:T(8,128)(2,1)}, bf16[384,1024]{1,0:T(8,128)(2,1)}, u32[]{:S(2)}, u32[]{:S(2)}) collective-permute-start(bf16[384,1024]{1,0:T(8,128)(2,1)} %pad_maximum_fusion.refs_11_.piece0), channel_id=1, source_target_pairs={{0,1},{1,0},{2,3},{3,2},{4,5},{5,4},{6,7},{7,6},{8,9},{9,8},{10,11... | collective-permute-start | bytes 2359304 | tf_op jit(solution)/shard_map/ppermute | solution.py:46
  84.2 54.0 %collective-permute-start.8 = (bf16[256,1024]{1,0:T(8,128)(2,1)}, bf16[256,1024]{1,0:T(8,128)(2,1)}, u32[]{:S(2)}, u32[]{:S(2)}) collective-permute-start(bf16[256,1024]{1,0:T(8,128)(2,1)} %refs_8_.1), channel_id=1, source_target_pairs={{0,1},{1,0},{2,3},{3,2},{4,5},{5,4},{6,7},{7,6},{8,9},{9,8},{10,11... | collective-permute-start | bytes 1572872 | tf_op jit(solution)/shard_map/ppermute | solution.py:46
  85.3 53.0 %collective-permute-start.9 = (bf16[256,1024]{1,0:T(8,128)(2,1)S(1)}, bf16[256,1024]{1,0:T(8,128)(2,1)}, u32[]{:S(2)}, u32[]{:S(2)}) collective-permute-start(bf16[256,1024]{1,0:T(8,128)(2,1)S(1)} %collective-permute-done.6.refs_5_.refs_4_.refs_10_), channel_id=1, source_target_pairs={{0,1},{1,0},{2,3},{3,2},{4,5},{5,4},{6,7},{7,6},{8,9},{9,8},{10,11... | collective-permute-start | bytes 1572872 | tf_op jit(solution)/shard_map/ppermute | solution.py:46
  85.4 52.8 %collective-permute-start.11 = (bf16[384,1024]{1,0:T(8,128)(2,1)}, bf16[384,1024]{1,0:T(8,128)(2,1)}, u32[]{:S(2)}, u32[]{:S(2)}) collective-permute-start(bf16[384,1024]{1,0:T(8,128)(2,1)} %collective-permute-done.7.refs_6_.refs_13_.piece2), channel_id=1, source_target_pairs={{0,1},{1,0},{2,3},{3,2},{4,5},{5,4},{6,7},{7,6},{8,9},{9,8},{10,11... | collective-permute-start | bytes 2359304 | tf_op jit(solution)/shard_map/ppermute | solution.py:46
  86.8 60.3 %copy-start.3 = (bf16[1,128,1024]{2,1,0:T(8,128)(2,1)S(1)}, bf16[1,128,1024]{2,1,0:T(8,128)(2,1)}, u32[]{:S(2)}) copy-start(bf16[1,128,1024]{2,1,0:T(8,128)(2,1)} %param.14) | copy-start | bytes 786436
  86.8 60.3 %copy-start.12 = (bf16[1024,32]{1,0:T(8,128)(2,1)S(1)}, bf16[1024,32]{1,0:T(8,128)(2,1)}, u32[]{:S(2)}) copy-start(bf16[1024,32]{1,0:T(8,128)(2,1)} %copy-done.11) | copy-start | bytes 196612
  131.7 15.4 %all-to-all-start.2 = ((bf16[8,128,128]{2,1,0:T(8,128)(2,1)}), bf16[8,128,128]{2,1,0:T(8,128)(2,1)}, u32[]{:S(2)}, u32[]{:S(2)}) async-start(bf16[8,128,128]{2,1,0:T(8,128)(2,1)} %bitcast.91), calls=%async_computation.2 | async-start | bytes 524288 | tf_op jit(solution)/shard_map/all_to_all | solution.py:58
  155.5 44.9 %all-to-all-start.3 = ((bf16[32,48,1024]{2,1,0:T(8,128)(2,1)}), bf16[32,48,1024]{2,1,0:T(8,128)(2,1)}, u32[]{:S(2)}, u32[]{:S(2)}) async-start(bf16[32,48,1024]{2,1,0:T(8,128)(2,1)} %bitcast.95), calls=%async_computation.3 | async-start | bytes 6291456 | tf_op jit(solution)/shard_map/all_to_all | solution.py:58
  164.2 64.7 %collective-permute-start.12 = (bf16[256,2048]{1,0:T(8,128)(2,1)}, bf16[256,2048]{1,0:T(8,128)(2,1)}, u32[]{:S(2)}, u32[]{:S(2)}) collective-permute-start(bf16[256,2048]{1,0:T(8,128)(2,1)} %add_dynamic-update-slice_fusion.1.refs_13_.refs_2_), channel_id=1, source_target_pairs={{0,2},{2,0},{1,3},{3,1},{4,6},{6,4},{5,7},{7,5},{8,10},{10,8},{9,1... | collective-permute-start | bytes 3145736 | tf_op jit(solution)/shard_map/ppermute | solution.py:46
  219.5 54.9 %all-to-all-start.4 = ((bf16[32,48,1152]{2,1,0:T(8,128)(2,1)}), bf16[32,48,1152]{2,1,0:T(8,128)(2,1)}, u32[]{:S(2)}, u32[]{:S(2)}) async-start(bf16[32,48,1152]{2,1,0:T(8,128)(2,1)} %bitcast.93), calls=%async_computation.4 | async-start | bytes 7077888 | tf_op jit(solution)/shard_map/all_to_all | solution.py:58
  230.3 12.0 %copy-start.52 = (s32[128,32]{0,1:T(8,128)S(1)}, s32[128,32]{0,1:T(8,128)}, u32[]{:S(2)}) copy-start(s32[128,32]{0,1:T(8,128)} %copy-done.51) | copy-start | bytes 49156
  241.6 5.2 %collective-permute-start.13 = (bf16[2,384,1024]{2,1,0:T(8,128)(2,1)}, bf16[2,384,1024]{2,1,0:T(8,128)(2,1)}, u32[]{:S(2)}, u32[]{:S(2)}) collective-permute-start(bf16[2,384,1024]{2,1,0:T(8,128)(2,1)} %get-tuple-element.88), channel_id=1, source_target_pairs={{0,1},{1,0},{2,3},{3,2},{4,5},{5,4},{6,7},{7,6},{8,9},{9,8},{10,11... | collective-permute-start | bytes 4718600 | tf_op jit(solution)/shard_map/ppermute | solution.py:46
  241.6 9.1 %collective-permute-start.14 = (bf16[256,2048]{1,0:T(8,128)(2,1)}, bf16[256,2048]{1,0:T(8,128)(2,1)}, u32[]{:S(2)}, u32[]{:S(2)}) collective-permute-start(bf16[256,2048]{1,0:T(8,128)(2,1)} %add_dynamic-update-slice_fusion.1.refs_13_.refs_2_), channel_id=1, source_target_pairs={{0,1},{1,0},{2,3},{3,2},{4,5},{5,4},{6,7},{7,6},{8,9},{9,8},{10,11... | collective-permute-start | bytes 3145736 | tf_op jit(solution)/shard_map/ppermute | solution.py:46
  242.1 8.6 %collective-permute-start.15 = (bf16[256,2048]{1,0:T(8,128)(2,1)}, bf16[256,2048]{1,0:T(8,128)(2,1)}, u32[]{:S(2)}, u32[]{:S(2)}) collective-permute-start(bf16[256,2048]{1,0:T(8,128)(2,1)} %collective-permute-done.12.refs_5_.refs_15_.refs_4_), channel_id=1, source_target_pairs={{0,1},{1,0},{2,3},{3,2},{4,5},{5,4},{6,7},{7,6},{8,9},{9,8},{10,11... | collective-permute-start | bytes 3145736 | tf_op jit(solution)/shard_map/ppermute | solution.py:46
  246.8 27.7 %copy-start = (bf16[128,1536]{1,0:T(8,128)(2,1)}, bf16[128,1536]{1,0:T(8,128)(2,1)S(1)}, u32[]{:S(2)}) copy-start(bf16[128,1536]{1,0:T(8,128)(2,1)S(1)} %compare_convert_fusion.refs_1_) | copy-start | bytes 1179652
  246.8 27.6 %copy-start.13 = (bf16[1024,32]{1,0:T(8,128)(2,1)S(1)}, bf16[1024,32]{1,0:T(8,128)(2,1)}, u32[]{:S(2)}) copy-start(bf16[1024,32]{1,0:T(8,128)(2,1)} %copy-done.11) | copy-start | bytes 196612
  277.2 4.6 copy-start.35
  277.3 4.6 copy-start.37
  283.7 6.0 %collective-permute-start.19 = (bf16[2,256,1152]{2,1,0:T(8,128)(2,1)S(1)}, bf16[2,256,1152]{2,1,0:T(8,128)(2,1)}, u32[]{:S(2)}, u32[]{:S(2)}) collective-permute-start(bf16[2,256,1152]{2,1,0:T(8,128)(2,1)S(1)} %get-tuple-element.102), channel_id=1, source_target_pairs={{0,1},{1,0},{2,3},{3,2},{4,5},{5,4},{6,7},{7,6},{8,9},{9,8},{10,11... | collective-permute-start | bytes 3538952 | tf_op jit(solution)/shard_map/ppermute | solution.py:46
  283.7 15.5 %all-to-all-start.5 = ((bf16[8,128,128]{2,1,0:T(8,128)(2,1)}), bf16[8,128,128]{2,1,0:T(8,128)(2,1)}, u32[]{:S(2)}, u32[]{:S(2)}) async-start(bf16[8,128,128]{2,1,0:T(8,128)(2,1)} %copy-done.24), calls=%async_computation.5 | async-start | bytes 524288 | tf_op jit(solution)/shard_map/all_to_all | solution.py:58
  289.7 9.5 %copy-start.39 = (s32[16]{0:T(128)S(1)}, s32[16]{0:T(128)}, u32[]{:S(2)}) copy-start(s32[16]{0:T(128)} %copy-done.38) | copy-start | bytes 196
  292.5 36.2 %collective-permute-start.20 = (bf16[256,1152]{1,0:T(8,128)(2,1)}, bf16[256,1152]{1,0:T(8,128)(2,1)}, u32[]{:S(2)}, u32[]{:S(2)}) collective-permute-start(bf16[256,1152]{1,0:T(8,128)(2,1)} %dynamic-slice_bitcast_fusion.1), channel_id=1, source_target_pairs={{0,2},{2,0},{1,3},{3,1},{4,6},{6,4},{5,7},{7,5},{8,10},{10,8},{9,1... | collective-permute-start | bytes 1769480 | tf_op jit(solution)/shard_map/ppermute | solution.py:46
  323.8 10.0 %collective-permute-start.16 = (bf16[1024,128]{1,0:T(8,128)(2,1)S(1)}, bf16[1024,128]{1,0:T(8,128)(2,1)S(1)}, u32[]{:S(2)}, u32[]{:S(2)}) collective-permute-start(bf16[1024,128]{1,0:T(8,128)(2,1)S(1)} %get-tuple-element.94), channel_id=1, source_target_pairs={{0,96},{32,0},{64,32},{96,64},{1,97},{33,1},{65,33},{97,65},{2,98}... | collective-permute-start | bytes 786440 | tf_op jit(solution)/shard_map/ppermute | solution.py:50
  327.1 12.4 %collective-permute-start.17 = (bf16[1024,128]{1,0:T(8,128)(2,1)S(1)}, bf16[1024,128]{1,0:T(8,128)(2,1)S(1)}, u32[]{:S(2)}, u32[]{:S(2)}) collective-permute-start(bf16[1024,128]{1,0:T(8,128)(2,1)S(1)} %get-tuple-element.95), channel_id=1, source_target_pairs={{0,64},{32,96},{64,0},{96,32},{1,65},{33,97},{65,1},{97,33},{2,66}... | collective-permute-start | bytes 786440 | tf_op jit(solution)/shard_map/ppermute | solution.py:50
  327.1 13.8 %collective-permute-start.18 = (bf16[1024,128]{1,0:T(8,128)(2,1)S(1)}, bf16[1024,128]{1,0:T(8,128)(2,1)S(1)}, u32[]{:S(2)}, u32[]{:S(2)}) collective-permute-start(bf16[1024,128]{1,0:T(8,128)(2,1)S(1)} %get-tuple-element.96), channel_id=1, source_target_pairs={{0,32},{32,64},{64,96},{96,0},{1,33},{33,65},{65,97},{97,1},{2,34}... | collective-permute-start | bytes 786440 | tf_op jit(solution)/shard_map/ppermute | solution.py:50
  330.1 13.6 %collective-permute-start.21 = (bf16[64,1152]{1,0:T(8,128)(2,1)S(1)}, bf16[64,1152]{1,0:T(8,128)(2,1)S(1)}, u32[]{:S(2)}, u32[]{:S(2)}) collective-permute-start(bf16[64,1152]{1,0:T(8,128)(2,1)S(1)} %get-tuple-element.104), channel_id=1, source_target_pairs={{0,32},{32,64},{64,96},{96,0},{1,33},{33,65},{65,97},{97,1},{2,34}... | collective-permute-start | bytes 442376 | tf_op jit(solution)/shard_map/ppermute | solution.py:50
  332.7 11.0 %collective-permute-start.22 = (bf16[64,1152]{1,0:T(8,128)(2,1)S(1)}, bf16[64,1152]{1,0:T(8,128)(2,1)S(1)}, u32[]{:S(2)}, u32[]{:S(2)}) collective-permute-start(bf16[64,1152]{1,0:T(8,128)(2,1)S(1)} %get-tuple-element.105), channel_id=1, source_target_pairs={{0,64},{32,96},{64,0},{96,32},{1,65},{33,97},{65,1},{97,33},{2,66}... | collective-permute-start | bytes 442376 | tf_op jit(solution)/shard_map/ppermute | solution.py:50
  333.8 10.4 %collective-permute-start.23 = (bf16[64,1152]{1,0:T(8,128)(2,1)S(1)}, bf16[64,1152]{1,0:T(8,128)(2,1)S(1)}, u32[]{:S(2)}, u32[]{:S(2)}) collective-permute-start(bf16[64,1152]{1,0:T(8,128)(2,1)S(1)} %get-tuple-element.106), channel_id=1, source_target_pairs={{0,96},{32,0},{64,32},{96,64},{1,97},{33,1},{65,33},{97,65},{2,98}... | collective-permute-start | bytes 442376 | tf_op jit(solution)/shard_map/ppermute | solution.py:50
  346.7 3.9 collective-permute-start.24
  346.8 18.9 %all-to-all-start.6 = ((bf16[8,176,256]{2,1,0:T(8,128)(2,1)}), bf16[8,176,256]{2,1,0:T(8,128)(2,1)S(1)}, u32[]{:S(2)}, u32[]{:S(2)}) async-start(bf16[8,176,256]{2,1,0:T(8,128)(2,1)} %get-tuple-element.107), calls=%async_computation.6 | async-start | bytes 1441792 | tf_op jit(solution)/shard_map/all_to_all | solution.py:58
  350.7 14.0 %collective-permute-start.25 = (bf16[256,256]{1,0:T(8,128)(2,1)S(1)}, bf16[256,256]{1,0:T(8,128)(2,1)S(1)}, u32[]{:S(2)}, u32[]{:S(2)}) collective-permute-start(bf16[256,256]{1,0:T(8,128)(2,1)S(1)} %dynamic-slice_bitcast_fusion.2), channel_id=1, source_target_pairs={{0,2},{2,0},{1,3},{3,1},{4,6},{6,4},{5,7},{7,5},{8,10},{10,8},{9,1... | collective-permute-start | bytes 393224 | tf_op jit(solution)/shard_map/ppermute | solution.py:46
  368.8 15.2 %copy-start.18 = (f32[128,1024]{1,0:T(8,128)S(1)}, f32[128,1024]{1,0:T(8,128)}, u32[]{:S(2)}) copy-start(f32[128,1024]{1,0:T(8,128)} %copy-done.17) | copy-start | bytes 1572868
  368.8 82.6 %all-to-all-start.7 = ((bf16[32,48,1024]{2,1,0:T(8,128)(2,1)}), bf16[32,48,1024]{2,1,0:T(8,128)(2,1)}, u32[]{:S(2)}, u32[]{:S(2)}) async-start(bf16[32,48,1024]{2,1,0:T(8,128)(2,1)} %bitcast.94), calls=%async_computation.7 | async-start | bytes 6291456 | tf_op jit(solution)/shard_map/all_to_all | solution.py:58
  384.0 6.0 %copy-start.45 = (bf16[2,384,1024]{2,1,0:T(8,128)(2,1)S(1)}, bf16[2,384,1024]{2,1,0:T(8,128)(2,1)}, u32[]{:S(2)}) copy-start(bf16[2,384,1024]{2,1,0:T(8,128)(2,1)} %add_convert_fusion.refs_12_) | copy-start | bytes 4718596
  390.1 61.3 %collective-permute-start.32 = (bf16[384,1024]{1,0:T(8,128)(2,1)S(1)}, bf16[384,1024]{1,0:T(8,128)(2,1)S(1)}, u32[]{:S(2)}, u32[]{:S(2)}) collective-permute-start(bf16[384,1024]{1,0:T(8,128)(2,1)S(1)} %dynamic-slice_bitcast_fusion), channel_id=1, source_target_pairs={{0,2},{2,0},{1,3},{3,1},{4,6},{6,4},{5,7},{7,5},{8,10},{10,8},{9,1... | collective-permute-start | bytes 2359304 | tf_op jit(solution)/shard_map/ppermute | solution.py:46
  390.2 2.2 collective-permute-start.26
  390.3 49.2 %collective-permute-start.27 = (f32[1,256]{1,0:T(1,128)S(1)}, f32[1,256]{1,0:T(1,128)S(1)}, u32[]{:S(2)}, u32[]{:S(2)}) collective-permute-start(f32[1,256]{1,0:T(1,128)S(1)} %get-tuple-element.116), channel_id=1, source_target_pairs={{0,2},{1,3},{2,0},{3,1},{4,6},{5,7},{6,4},{7,5},{8,10},{9,11},{10,... | collective-permute-start | bytes 3080 | tf_op jit(solution)/shard_map/ppermute | solution.py:896
  392.2 47.3 %collective-permute-start.28 = (f32[1,256]{1,0:T(1,128)S(1)}, f32[1,256]{1,0:T(1,128)S(1)}, u32[]{:S(2)}, u32[]{:S(2)}) collective-permute-start(f32[1,256]{1,0:T(1,128)S(1)} %get-tuple-element.117), channel_id=1, source_target_pairs={{0,3},{1,2},{2,1},{3,0},{4,7},{5,6},{6,5},{7,4},{8,11},{9,10},{10,... | collective-permute-start | bytes 3080 | tf_op jit(solution)/shard_map/ppermute | solution.py:896
  439.5 7.6 %collective-permute-start.29 = (bf16[80,1152]{1,0:T(8,128)(2,1)S(1)}, bf16[80,1152]{1,0:T(8,128)(2,1)S(1)}, u32[]{:S(2)}, u32[]{:S(2)}) collective-permute-start(bf16[80,1152]{1,0:T(8,128)(2,1)S(1)} %shard_map.245.refs_1_), channel_id=1, source_target_pairs={{0,32},{32,64},{64,96},{96,0},{1,33},{33,65},{65,97},{97,1},{2,34}... | collective-permute-start | bytes 552968 | tf_op jit(solution)/shard_map/ppermute | solution.py:50
  439.6 9.1 %collective-permute-start.30 = (bf16[80,1152]{1,0:T(8,128)(2,1)S(1)}, bf16[80,1152]{1,0:T(8,128)(2,1)S(1)}, u32[]{:S(2)}, u32[]{:S(2)}) collective-permute-start(bf16[80,1152]{1,0:T(8,128)(2,1)S(1)} %shard_map.245.refs_1_), channel_id=1, source_target_pairs={{0,64},{32,96},{64,0},{96,32},{1,65},{33,97},{65,1},{97,33},{2,66}... | collective-permute-start | bytes 552968 | tf_op jit(solution)/shard_map/ppermute | solution.py:50
  441.2 10.2 %collective-permute-start.31 = (bf16[80,1152]{1,0:T(8,128)(2,1)S(1)}, bf16[80,1152]{1,0:T(8,128)(2,1)S(1)}, u32[]{:S(2)}, u32[]{:S(2)}) collective-permute-start(bf16[80,1152]{1,0:T(8,128)(2,1)S(1)} %shard_map.245.refs_1_), channel_id=1, source_target_pairs={{0,96},{32,0},{64,32},{96,64},{1,97},{33,1},{65,33},{97,65},{2,98}... | collective-permute-start | bytes 552968 | tf_op jit(solution)/shard_map/ppermute | solution.py:50
  452.9 7.0 %copy-start.23 = (f32[128,32]{1,0:T(8,128)S(1)}, f32[128,32]{1,0:T(8,128)}, u32[]{:S(2)}) copy-start(f32[128,32]{1,0:T(8,128)} %copy-done.21) | copy-start | bytes 49156
  452.9 32.1 %all-to-all-start.8 = ((bf16[8,96,1152]{2,1,0:T(8,128)(2,1)}), bf16[8,96,1152]{2,1,0:T(8,128)(2,1)S(1)}, u32[]{:S(2)}, u32[]{:S(2)}) async-start(bf16[8,96,1152]{2,1,0:T(8,128)(2,1)} %shard_map.246), calls=%async_computation.8 | async-start | bytes 3538944 | tf_op jit(solution)/shard_map/all_to_all | solution.py:58
  (38 other events, 42.5 us)
where the time goes:
time: 498 us; the launch traced here: 488 us
  waiting for transfers between devices  200 us (40%)
  Pallas kernels  107 us (21%)
  starting transfers between devices  106 us (21%)
  local copies, waits for them, and re-layouts  47.2 us (9%)
  other arithmetic  17.1 us (3%)
  matrix products  6.01 us (1%)
  between operations  5.06 us (1%)
    all_to_all x9, waiting for transfers between devices, exchange(): lax.all_to_all(rows_first(values), axes, 0, 0, tiled=True)  102 us
    all_to_all x9, starting transfers between devices, exchange(): lax.all_to_all(rows_first(values), axes, 0, 0, tiled=True)  73 us
    ppermute x3, waiting for transfers between devices, on_device(): lax.ppermute(gain_parts[step], ('yl', 'core'), [(i, i ^ step) for i in ra...  47.2 us
    pallas_call x15, Pallas kernels, call(): pl.pallas_call(body, grid=(1,), out_shape=tuple((jax.ShapeDtypeStruct(sha...  38.1 us
    unnamed x122, local copies, waits for them, and re-layouts  24.6 us
    pallas_call x1, Pallas kernels, attend(): pl.pallas_call(attend_kernel, grid=(1,), out_shape=outs, in_specs=[SMEM]...  23.3 us
    ppermute x15, waiting for transfers between devices, swap(): return lax.ppermute(values, axis, [(0, 1), (1, 0)])  22.7 us
    pallas_call x1, Pallas kernels, attend_grad(): pl.pallas_call(attend_grad_kernel, grid=(1,), out_shape=outs, in_specs=[S...  21.9 us
  transfers between devices with their start and end apart: 42, of which 20 were waited for; matrix products, arithmetic and copies ran while one was open for 9% of the time, Pallas kernels for 18%

commit v1 on v0

--- a/solution.py
+++ b/solution.py
@@ -763,8 +763,6 @@
     kv_parts = [kv_own] + [turn(kv_own, "x", step) for step in (1, 2, 3)]
 
     out_other = swap(w_out, "yl")
-    expert_shard = jnp.concatenate([jnp.concatenate([w_gate[0], w_up[0]], axis=1), w_down[0]], axis=0)
-    expert_other = swap(expert_shard, "yl")
     marked = jnp.concatenate(
         [cotangent[0], uses.astype(bf16), jnp.zeros((tokens, 128 - EXPERTS), bf16)], axis=1
     )
@@ -773,16 +771,19 @@
         [((EXPERTS * CAP, width + 128), bf16)],
         (send, marked),
         500_000_000,
-        held=(*kv_parts[1:], out_other, expert_other),
+        held=(*kv_parts[1:], out_other),
     )
     marked_arrived = exchange(marked_sent, CTX)
 
     attn_group, attn_turned, lse = attend(numbers, queries, kv_parts)
 
     out_pieces = pieces_by_row(w_out, out_other)
+    expert_shard = jnp.concatenate([jnp.concatenate([w_gate[0], w_up[0]], axis=1), w_down[0]], axis=0)
+    expert_shard = tie(expert_shard, attn_group)
+    expert_row = swap(expert_shard, "yl")
 
     attn_back = exchange(tie(attn_group, marked_arrived), ZY)
-    expert_pieces = pieces_by_row(expert_shard, expert_other)
+    expert_pieces = pieces_by_row(expert_shard, expert_row)
     attn_rows, hidden, normed2, gate_probs, outgoing = call(
         middle_kernel,
         [
@@ -797,7 +798,7 @@
             uses, send,
         ),
         800_000_000,
-        held=expert_pieces,
+        held=(expert_row,),
         scalars=1,
     )
     arrived = exchange(outgoing, CTX)
@@ -873,8 +874,6 @@
     )
     head_part = scatter_row(head_both).astype(bf16)
 
-    returned = exchange(tie(expert_out, token_grads, head_part), CTX)
-
 
     gain_shape = ((1, shard_rows), f32)
     input_grad, *gain_parts, dense = call(
@@ -887,11 +886,6 @@
         scalars=1,
         scratch=[(1, width)],
     )
-    later = (gain_parts[0][0, 0] * 0.0).astype(jnp.int32)
-    expert_away = lax.dynamic_slice_in_dim(expert_both, 1 - row[0] + later, 1, 0)[0]
-    expert_other = swap(expert_away, "yl")
-    expert_sums = lax.dynamic_index_in_dim(expert_both, row[0], 0, keepdims=False).astype(f32)
-    expert_sums = expert_sums + expert_other.astype(f32)
     gain_turned = [
         lax.ppermute(gain_parts[step], ("yl", "core"), [(i, i ^ step) for i in range(4)]) for step in (1, 2, 3)
     ]
@@ -901,10 +895,17 @@
         (head_part, gain_parts[0], *gain_turned, dense),
         1_000_000,
     )
+    lines = all_x(line)
+    returned = exchange(tie(expert_out, line), CTX)
+    later = (line[0, 0].astype(f32) * 0.0).astype(jnp.int32)
+    expert_away = lax.dynamic_slice_in_dim(expert_both, 1 - row[0] + later, 1, 0)[0]
+    expert_other = swap(expert_away, "yl")
+    expert_sums = lax.dynamic_index_in_dim(expert_both, row[0], 0, keepdims=False).astype(f32)
+    expert_sums = expert_sums + expert_other.astype(f32)
     (last,) = call(
         pack_kernel,
         [((KV_HEADS, shard_rows // 4 + 32, width + 128), bf16)],
-        (place, *all_x(line)),
+        (place, *lines),
         1_000_000,
         held=(returned, expert_other),
         scalars=1,

time: 498 us -> 502 us (level)
  the two profiles are of different devices: /device:TPU:2 before, /device:TPU:0 now
where the time goes in v1:
time: 502 us; the launch traced here: 496 us
  waiting for transfers between devices  195 us (39%)
  starting transfers between devices  116 us (23%)
  Pallas kernels  106 us (21%)
  local copies, waits for them, and re-layouts  48 us (10%)
  other arithmetic  20.5 us (4%)
  matrix products  6 us (1%)
    all_to_all x9, waiting for transfers between devices, exchange(): lax.all_to_all(rows_first(values), axes, 0, 0, tiled=True)  107 us
    all_to_all x9, starting transfers between devices, exchange(): lax.all_to_all(rows_first(values), axes, 0, 0, tiled=True)  66.9 us
    ppermute x12, waiting for transfers between devices, turn(): return lax.ppermute(values, axis, [(i, (i + step) % 4) for i in range(4)])  63.3 us
    pallas_call x15, Pallas kernels, call(): pl.pallas_call(body, grid=(1,), out_shape=tuple((jax.ShapeDtypeStruct(sha...  38 us
    ppermute x12, starting transfers between devices, turn(): return lax.ppermute(values, axis, [(i, (i + step) % 4) for i in range(4)])  24.3 us
    pallas_call x1, Pallas kernels, attend(): pl.pallas_call(attend_kernel, grid=(1,), out_shape=outs, in_specs=[SMEM]...  23.4 us
    unnamed x116, local copies, waits for them, and re-layouts  23.3 us
    pallas_call x1, Pallas kernels, attend_grad(): pl.pallas_call(attend_grad_kernel, grid=(1,), out_shape=outs, in_specs=[S...  21.4 us
  transfers between devices with their start and end apart: 42, of which 21 were waited for; matrix products, arithmetic and copies ran while one was open for 10% of the time, Pallas kernels for 17%

profile of v1, /device:TPU:0, one launch (start us, length us, event | category | flops | bytes accessed | tf_op | source)
XLA Modules:
  0.0 495.6 jit_solution(7316823876673211043)
XLA Ops:
  1.6 1.5 shard_map.229
  3.1 8.2 %all-to-all-start = ((bf16[8,128,1024]{2,1,0:T(8,128)(2,1)}), bf16[8,128,1024]{2,1,0:T(8,128)(2,1)}, u32[]{:S(2)}, u32[]{:S(2)}) async-start(bf16[8,128,1024]{2,1,0:T(8,128)(2,1)} %shard_map.229), calls=%async_computation | async-start | bytes 4194304 | tf_op jit(solution)/shard_map/all_to_all | solution.py:58
  16.8 3.1 multiply_sine_fusion
  19.9 3.3 concatenate.22.cos_ref.refs_5_
  23.9 3.8 concatenate.24.sin_ref.refs_6_
  27.8 11.9 %collective-permute-done.1.refs_3_ = bf16[304,256]{1,0:T(8,128)(2,1)S(1)} collective-permute-done((bf16[304,256]{1,0:T(8,128)(2,1)S(1)}, bf16[304,256]{1,0:T(8,128)(2,1)S(1)}, u32[]{:S(2)}, u32[]{:S(2)}) %collective-permute-start.1) | collective-permute-done | bytes 155680 | tf_op jit(solution)/shard_map/ppermute | solution.py:71
  40.3 1.7 collective-permute-done.2.refs_4_
  45.4 4.5 shard_map.232
  52.0 1.5 collective-permute-start.3
  53.5 2.7 collective-permute-start.4
  56.2 1.4 collective-permute-start.5
  60.0 2.5 collective-permute-done.3.kv1.refs_2_
  62.5 6.6 %collective-permute-done.4.kv2.refs_3_ = bf16[1024,128]{1,0:T(8,128)(2,1)} collective-permute-done((bf16[1024,128]{1,0:T(8,128)(2,1)}, bf16[1024,128]{1,0:T(8,128)(2,1)}, u32[]{:S(2)}, u32[]{:S(2)}) %collective-permute-start.4) | collective-permute-done | bytes 262176 | tf_op jit(solution)/shard_map/ppermute | solution.py:50
  69.1 2.9 shard_map.234
  72.0 10.4 %all-to-all-start.1 = ((bf16[32,48,1152]{2,1,0:T(8,128)(2,1)}), bf16[32,48,1152]{2,1,0:T(8,128)(2,1)}, u32[]{:S(2)}, u32[]{:S(2)}) async-start(bf16[32,48,1152]{2,1,0:T(8,128)(2,1)} %bitcast.12), calls=%async_computation.1 | async-start | bytes 7077888 | tf_op jit(solution)/shard_map/all_to_all | solution.py:58
  86.2 1.9 pad_maximum_fusion
  89.1 23.4 %shard_map.233 = (bf16[1024,128]{1,0:T(8,128)(2,1)}, f32[8,64,256]{2,1,0:T(8,128)S(1)}, f32[8,1,256]{2,1,0:T(1,128)S(1)}) custom-call(s32[16]{0:T(128)S(1)} %select_reduce_fusion.order_ref, s32[16]{0:T(128)S(1)} %lt.40.qnum_ref, s32[64]{0:T(128)S(1)} %reshape.203.knum_ref, bf16[1024,128]{1,0:T(8,128)(2,1)S(1)} %copy-done.31, ...), custom_call_target="tpu_custom_call" | custom-call | flops 12000000000 | bytes 4000000 | tf_op jit(solution)/shard_map/pallas_call | solution.py:656
  117.6 12.4 %all-to-all-done.1 = bf16[32,48,1152]{2,1,0:T(8,128)(2,1)} async-done(((bf16[32,48,1152]{2,1,0:T(8,128)(2,1)}), bf16[32,48,1152]{2,1,0:T(8,128)(2,1)}, u32[]{:S(2)}, u32[]{:S(2)}) %all-to-all-start.1) | async-done | bytes 3538976 | tf_op jit(solution)/shard_map/all_to_all | solution.py:58
  132.9 6.6 %all-to-all-start.2 = ((bf16[8,128,128]{2,1,0:T(8,128)(2,1)}), bf16[8,128,128]{2,1,0:T(8,128)(2,1)}, u32[]{:S(2)}, u32[]{:S(2)}) async-start(bf16[8,128,128]{2,1,0:T(8,128)(2,1)} %bitcast.15), calls=%async_computation.2 | async-start | bytes 524288 | tf_op jit(solution)/shard_map/all_to_all | solution.py:58
  139.6 2.9 collective-permute-done.9.refs_11_.piece2
  142.5 6.7 %all-to-all-done.2.refs_1_ = bf16[8,128,128]{2,1,0:T(8,128)(2,1)} async-done(((bf16[8,128,128]{2,1,0:T(8,128)(2,1)}), bf16[8,128,128]{2,1,0:T(8,128)(2,1)}, u32[]{:S(2)}, u32[]{:S(2)}) %all-to-all-start.2) | async-done | bytes 262176 | tf_op jit(solution)/shard_map/all_to_all | solution.py:58
  150.0 4.7 shard_map.235
  157.5 6.9 %all-to-all-start.3 = ((bf16[32,48,1024]{2,1,0:T(8,128)(2,1)}), bf16[32,48,1024]{2,1,0:T(8,128)(2,1)}, u32[]{:S(2)}, u32[]{:S(2)}) async-start(bf16[32,48,1024]{2,1,0:T(8,128)(2,1)} %bitcast.93), calls=%async_computation.3 | async-start | bytes 6291456 | tf_op jit(solution)/shard_map/all_to_all | solution.py:58
  168.3 1.6 collective-permute-start.12
  169.9 35.9 %all-to-all-done.3 = bf16[32,48,1024]{2,1,0:T(8,128)(2,1)} async-done(((bf16[32,48,1024]{2,1,0:T(8,128)(2,1)}), bf16[32,48,1024]{2,1,0:T(8,128)(2,1)}, u32[]{:S(2)}, u32[]{:S(2)}) %all-to-all-start.3) | async-done | bytes 3145760 | tf_op jit(solution)/shard_map/all_to_all | solution.py:58
  205.9 19.2 %shard_map.236 = (bf16[1536,1024]{1,0:T(8,128)(2,1)}, bf16[1536,1152]{1,0:T(8,128)(2,1)}, bf16[1536,1024]{1,0:T(8,128)(2,1)}, bf16[1536,512]{1,0:T(8,128)(2,1)}, bf16[1536,1024]{1,0:T(8,128)(2,1)}) custom-call(s32[1]{0:T(128)} %bitcast.24.expert_ref, s32[1]{0:T(128)} %bitcast.refs_0_.me_ref, bf16[1536,1024]{1,0:T(8,128)(2,1)} %bitcast.26.rows_ref.refs_1_, ...), custom_call_target="tpu_custom_call" | custom-call | flops 10000000000 | bytes 22000000 | tf_op jit(solution)/shard_map/pallas_call | solution.py:628
  225.0 8.6 %all-to-all-start.4 = ((bf16[32,48,1152]{2,1,0:T(8,128)(2,1)}), bf16[32,48,1152]{2,1,0:T(8,128)(2,1)}, u32[]{:S(2)}, u32[]{:S(2)}) async-start(bf16[32,48,1152]{2,1,0:T(8,128)(2,1)} %bitcast.91), calls=%async_computation.4 | async-start | bytes 7077888 | tf_op jit(solution)/shard_map/all_to_all | solution.py:58
  235.1 10.1 %shard_map.237 = (bf16[2,384,1024]{2,1,0:T(8,128)(2,1)S(1)}, bf16[2,384,1024]{2,1,0:T(8,128)(2,1)}) custom-call(s32[1]{0:T(128)} %bitcast.27.refs_0_, bf16[1536,1024]{1,0:T(8,128)(2,1)} %bitcast.26.rows_ref.refs_1_, bf16[1536,1024]{1,0:T(8,128)(2,1)} %get-tuple-element.83.refs_2_, bf16[1536,512]{1,0:T(8,128)(2,1)S(1)} %copy-done.39, ...), custom_call_target="tpu_custom_call" | custom-call | flops 5000000000 | bytes 8000000 | tf_op jit(solution)/shard_map/pallas_call | solution.py:349
  247.8 2.3 copy.60
  251.3 3.9 add_convert_fusion.refs_12_
  255.2 24.2 %all-to-all-done.4 = bf16[32,48,1152]{2,1,0:T(8,128)(2,1)} async-done(((bf16[32,48,1152]{2,1,0:T(8,128)(2,1)}), bf16[32,48,1152]{2,1,0:T(8,128)(2,1)}, u32[]{:S(2)}, u32[]{:S(2)}) %all-to-all-start.4) | async-done | bytes 3538976 | tf_op jit(solution)/shard_map/all_to_all | solution.py:58
  282.3 4.5 shard_map.238
  288.7 9.6 %collective-permute-start.19 = (bf16[2,256,1152]{2,1,0:T(8,128)(2,1)S(1)}, bf16[2,256,1152]{2,1,0:T(8,128)(2,1)}, u32[]{:S(2)}, u32[]{:S(2)}) collective-permute-start(bf16[2,256,1152]{2,1,0:T(8,128)(2,1)S(1)} %get-tuple-element.103), channel_id=1, source_target_pairs={{0,1},{1,0},{2,3},{3,2},{4,5},{5,4},{6,7},{7,6},{8,9},{9,8},{10,11... | collective-permute-start | bytes 3538952 | tf_op jit(solution)/shard_map/ppermute | solution.py:46
  298.3 5.7 %all-to-all-start.5 = ((bf16[8,128,128]{2,1,0:T(8,128)(2,1)}), bf16[8,128,128]{2,1,0:T(8,128)(2,1)}, u32[]{:S(2)}, u32[]{:S(2)}) async-start(bf16[8,128,128]{2,1,0:T(8,128)(2,1)} %copy-done.23), calls=%async_computation.5 | async-start | bytes 524288 | tf_op jit(solution)/shard_map/all_to_all | solution.py:58
  304.0 1.9 add_convert_fusion.1.refs_2_
  306.8 4.0 collective-permute-start.20
  310.8 2.7 all-to-all-done.5
  316.2 21.4 %shard_map.239 = (f32[1024,128]{1,0:T(8,128)S(1)}, bf16[1024,128]{1,0:T(8,128)(2,1)S(1)}, bf16[1024,128]{1,0:T(8,128)(2,1)S(1)}, bf16[1024,128]{1,0:T(8,128)(2,1)S(1)}, bf16[1024,128]{1,0:T(8,128)(2,1)S(1)}) custom-call(s32[16]{0:T(128)S(1)} %copy-done.38, s32[16]{0:T(128)S(1)} %lt.40.qnum_ref, s32[64]{0:T(128)S(1)} %reshape.203.knum_ref, ...), custom_call_target="tpu_custom_call" | custom-call | flops 30000001024 | bytes 6000000 | tf_op jit(solution)/shard_map/pallas_call | solution.py:673
  337.6 4.0 collective-permute-start.16
  342.6 1.5 shard_map.241
  344.1 2.6 collective-permute-start.21
  348.1 7.4 %collective-permute-done.16.refs_2_ = bf16[1024,128]{1,0:T(8,128)(2,1)S(1)} collective-permute-done((bf16[1024,128]{1,0:T(8,128)(2,1)S(1)}, bf16[1024,128]{1,0:T(8,128)(2,1)S(1)}, u32[]{:S(2)}, u32[]{:S(2)}) %collective-permute-start.16) | collective-permute-done | bytes 262176 | tf_op jit(solution)/shard_map/ppermute | solution.py:50
  355.6 3.7 collective-permute-start.23
  360.5 1.9 collective-permute-done.22.refs_9_
  362.5 1.7 shard_map.242
  365.0 4.9 all-to-all-start.6
  370.1 2.3 collective-permute-start.25
  372.4 12.7 %all-to-all-done.6.refs_1_ = bf16[8,176,256]{2,1,0:T(8,128)(2,1)S(1)} async-done(((bf16[8,176,256]{2,1,0:T(8,128)(2,1)}), bf16[8,176,256]{2,1,0:T(8,128)(2,1)S(1)}, u32[]{:S(2)}, u32[]{:S(2)}) %all-to-all-start.6) | async-done | bytes 720928 | tf_op jit(solution)/shard_map/all_to_all | solution.py:58
  385.1 4.7 shard_map.244
  389.8 2.1 collective-permute-start.27
  393.4 1.4 collective-permute-done.28.refs_4_
  397.2 6.2 %all-to-all-start.7 = ((bf16[32,48,1024]{2,1,0:T(8,128)(2,1)}), bf16[32,48,1024]{2,1,0:T(8,128)(2,1)}, u32[]{:S(2)}, u32[]{:S(2)}) async-start(bf16[32,48,1024]{2,1,0:T(8,128)(2,1)} %bitcast.92), calls=%async_computation.7 | async-start | bytes 6291456 | tf_op jit(solution)/shard_map/all_to_all | solution.py:58
  403.6 1.8 collective-permute-start.29
  405.4 2.7 collective-permute-start.30
  408.1 1.4 collective-permute-start.31
  409.5 38.0 %collective-permute-done.29.refs_2_ = bf16[80,1152]{1,0:T(8,128)(2,1)S(1)} collective-permute-done((bf16[80,1152]{1,0:T(8,128)(2,1)S(1)}, bf16[80,1152]{1,0:T(8,128)(2,1)S(1)}, u32[]{:S(2)}, u32[]{:S(2)}) %collective-permute-start.29) | collective-permute-done | bytes 184352 | tf_op jit(solution)/shard_map/ppermute | solution.py:50
  447.5 5.5 %collective-permute-done.30.refs_3_ = bf16[80,1152]{1,0:T(8,128)(2,1)S(1)} collective-permute-done((bf16[80,1152]{1,0:T(8,128)(2,1)S(1)}, bf16[80,1152]{1,0:T(8,128)(2,1)S(1)}, u32[]{:S(2)}, u32[]{:S(2)}) %collective-permute-start.30) | collective-permute-done | bytes 184352 | tf_op jit(solution)/shard_map/ppermute | solution.py:50
  453.2 4.8 collective-permute-done.32.refs_6_
  457.9 1.5 shard_map.246
  459.4 9.4 %all-to-all-start.8 = ((bf16[8,96,1152]{2,1,0:T(8,128)(2,1)}), bf16[8,96,1152]{2,1,0:T(8,128)(2,1)S(1)}, u32[]{:S(2)}, u32[]{:S(2)}) async-start(bf16[8,96,1152]{2,1,0:T(8,128)(2,1)} %shard_map.246), calls=%async_computation.8 | async-start | bytes 3538944 | tf_op jit(solution)/shard_map/all_to_all | solution.py:58
  474.5 2.5 fusion.7
  477.1 3.2 fusion.3
  480.3 12.5 %all-to-all-done.8.refs_0_ = bf16[8,96,1152]{2,1,0:T(8,128)(2,1)S(1)} async-done(((bf16[8,96,1152]{2,1,0:T(8,128)(2,1)}), bf16[8,96,1152]{2,1,0:T(8,128)(2,1)S(1)}, u32[]{:S(2)}, u32[]{:S(2)}) %all-to-all-start.8) | async-done | bytes 1769504 | tf_op jit(solution)/shard_map/all_to_all | solution.py:58
  492.9 1.8 shard_map.247
  (216 shorter events, 62.3 us)
Async XLA Ops:
  3.1 8.2 %copy-start.52 = (bf16[256,32]{0,1:T(8,128)(2,1)S(1)}, bf16[256,32]{0,1:T(8,128)(2,1)}, u32[]{:S(2)}) copy-start(bf16[256,32]{0,1:T(8,128)(2,1)} %param.23) | copy-start | bytes 49156
  3.1 8.3 %copy-start.55 = (bf16[256]{0:T(256)(128)(2,1)S(1)}, bf16[256]{0:T(256)(128)(2,1)}, u32[]{:S(2)}) copy-start(bf16[256]{0:T(256)(128)(2,1)} %param.17) | copy-start | bytes 1540
  3.1 8.4 %copy-start.56 = (bf16[256]{0:T(256)(128)(2,1)S(1)}, bf16[256]{0:T(256)(128)(2,1)}, u32[]{:S(2)}) copy-start(bf16[256]{0:T(256)(128)(2,1)} %param.22) | copy-start | bytes 1540
  3.1 8.4 %copy-start.19 = (bf16[256,1024]{1,0:T(8,128)(2,1)S(1)}, bf16[256,1024]{1,0:T(8,128)(2,1)}, u32[]{:S(2)}) copy-start(bf16[256,1024]{1,0:T(8,128)(2,1)} %refs_1_.1) | copy-start | bytes 1572868
  3.1 8.4 %copy-start.24 = (bf16[256,512]{1,0:T(8,128)(2,1)S(1)}, bf16[256,512]{1,0:T(8,128)(2,1)}, u32[]{:S(2)}) copy-start(bf16[256,512]{1,0:T(8,128)(2,1)} %refs_2_.2) | copy-start | bytes 786436
  3.1 8.4 %copy-start.25 = (bf16[256,512]{1,0:T(8,128)(2,1)S(1)}, bf16[256,512]{1,0:T(8,128)(2,1)}, u32[]{:S(2)}) copy-start(bf16[256,512]{1,0:T(8,128)(2,1)} %refs_3_.1) | copy-start | bytes 786436
  3.1 12.2 %copy-start.54 = (s32[32]{0:T(128)S(1)}, s32[32]{0:T(128)}, u32[]{:S(2)}) copy-start(s32[32]{0:T(128)} %param.16) | copy-start | bytes 388
  3.1 42.3 %all-to-all-start = ((bf16[8,128,1024]{2,1,0:T(8,128)(2,1)}), bf16[8,128,1024]{2,1,0:T(8,128)(2,1)}, u32[]{:S(2)}, u32[]{:S(2)}) async-start(bf16[8,128,1024]{2,1,0:T(8,128)(2,1)} %shard_map.229), calls=%async_computation | async-start | bytes 4194304 | tf_op jit(solution)/shard_map/all_to_all | solution.py:58
  12.8 15.0 %collective-permute-start = (bf16[304,256]{1,0:T(8,128)(2,1)S(1)}, bf16[304,256]{1,0:T(8,128)(2,1)S(1)}, u32[]{:S(2)}, u32[]{:S(2)}) collective-permute-start(bf16[304,256]{1,0:T(8,128)(2,1)S(1)} %get-tuple-element.69.refs_1_), channel_id=1, source_target_pairs={{0,1},{1,0},{2,3},{3,2},{4,5},{5,4},{6,7},{7,6},{8,9},{9,8},{10,11... | collective-permute-start | bytes 466952 | tf_op jit(solution)/shard_map/ppermute | solution.py:71
  12.8 26.8 %collective-permute-start.1 = (bf16[304,256]{1,0:T(8,128)(2,1)S(1)}, bf16[304,256]{1,0:T(8,128)(2,1)S(1)}, u32[]{:S(2)}, u32[]{:S(2)}) collective-permute-start(bf16[304,256]{1,0:T(8,128)(2,1)S(1)} %get-tuple-element.69.refs_1_), channel_id=1, source_target_pairs={{0,2},{1,3},{2,0},{3,1},{4,6},{5,7},{6,4},{7,5},{8,10},{9,11},{10,... | collective-permute-start | bytes 466952 | tf_op jit(solution)/shard_map/ppermute | solution.py:71
  13.5 28.5 %collective-permute-start.2 = (bf16[304,256]{1,0:T(8,128)(2,1)S(1)}, bf16[304,256]{1,0:T(8,128)(2,1)S(1)}, u32[]{:S(2)}, u32[]{:S(2)}) collective-permute-start(bf16[304,256]{1,0:T(8,128)(2,1)S(1)} %get-tuple-element.69.refs_1_), channel_id=1, source_target_pairs={{0,3},{1,2},{2,1},{3,0},{4,7},{5,6},{6,5},{7,4},{8,11},{9,10},{10,... | collective-permute-start | bytes 466952 | tf_op jit(solution)/shard_map/ppermute | solution.py:71
  14.7 45.4 %collective-permute-start.6 = (bf16[256,1024]{1,0:T(8,128)(2,1)}, bf16[256,1024]{1,0:T(8,128)(2,1)S(1)}, u32[]{:S(2)}, u32[]{:S(2)}) collective-permute-start(bf16[256,1024]{1,0:T(8,128)(2,1)} %refs_8_.1), channel_id=1, source_target_pairs={{0,2},{2,0},{1,3},{3,1},{4,6},{6,4},{5,7},{7,5},{8,10},{10,8},{9,1... | collective-permute-start | bytes 1572872 | tf_op jit(solution)/shard_map/ppermute | solution.py:46
  23.9 3.8 copy-start.53
  52.0 10.5 %collective-permute-start.3 = (bf16[1024,128]{1,0:T(8,128)(2,1)}, bf16[1024,128]{1,0:T(8,128)(2,1)}, u32[]{:S(2)}, u32[]{:S(2)}) collective-permute-start(bf16[1024,128]{1,0:T(8,128)(2,1)} %get-tuple-element.73.kv0), channel_id=1, source_target_pairs={{0,32},{32,64},{64,96},{96,0},{1,33},{33,65},{65,97},{97,1},{2,34}... | collective-permute-start | bytes 786440 | tf_op jit(solution)/shard_map/ppermute | solution.py:50
  53.5 15.6 %collective-permute-start.4 = (bf16[1024,128]{1,0:T(8,128)(2,1)}, bf16[1024,128]{1,0:T(8,128)(2,1)}, u32[]{:S(2)}, u32[]{:S(2)}) collective-permute-start(bf16[1024,128]{1,0:T(8,128)(2,1)} %get-tuple-element.73.kv0), channel_id=1, source_target_pairs={{0,64},{32,96},{64,0},{96,32},{1,65},{33,97},{65,1},{97,33},{2,66}... | collective-permute-start | bytes 786440 | tf_op jit(solution)/shard_map/ppermute | solution.py:50
  56.2 12.9 %collective-permute-start.5 = (bf16[1024,128]{1,0:T(8,128)(2,1)}, bf16[1024,128]{1,0:T(8,128)(2,1)}, u32[]{:S(2)}, u32[]{:S(2)}) collective-permute-start(bf16[1024,128]{1,0:T(8,128)(2,1)} %get-tuple-element.73.kv0), channel_id=1, source_target_pairs={{0,96},{32,0},{64,32},{96,64},{1,97},{33,1},{65,33},{97,65},{2,98}... | collective-permute-start | bytes 786440 | tf_op jit(solution)/shard_map/ppermute | solution.py:50
  72.0 14.2 %copy-start.45 = (bf16[1,256,512]{2,1,0:T(8,128)(2,1)S(1)}, bf16[1,256,512]{2,1,0:T(8,128)(2,1)}, u32[]{:S(2)}) copy-start(bf16[1,256,512]{2,1,0:T(8,128)(2,1)} %param.24) | copy-start | bytes 786436
  72.0 14.2 %copy-start.46 = (bf16[1,128,1024]{2,1,0:T(8,128)(2,1)S(1)}, bf16[1,128,1024]{2,1,0:T(8,128)(2,1)}, u32[]{:S(2)}) copy-start(bf16[1,128,1024]{2,1,0:T(8,128)(2,1)} %param.26) | copy-start | bytes 786436
  72.0 57.9 %all-to-all-start.1 = ((bf16[32,48,1152]{2,1,0:T(8,128)(2,1)}), bf16[32,48,1152]{2,1,0:T(8,128)(2,1)}, u32[]{:S(2)}, u32[]{:S(2)}) async-start(bf16[32,48,1152]{2,1,0:T(8,128)(2,1)} %bitcast.12), calls=%async_computation.1 | async-start | bytes 7077888 | tf_op jit(solution)/shard_map/all_to_all | solution.py:58
  86.2 26.3 %copy-start.37 = (s32[16]{0:T(128)}, s32[16]{0:T(128)S(1)}, u32[]{:S(2)}) copy-start(s32[16]{0:T(128)S(1)} %select_reduce_fusion.order_ref) | copy-start | bytes 196
  89.1 60.1 %copy-start.3 = (bf16[1,128,1024]{2,1,0:T(8,128)(2,1)S(1)}, bf16[1,128,1024]{2,1,0:T(8,128)(2,1)}, u32[]{:S(2)}) copy-start(bf16[1,128,1024]{2,1,0:T(8,128)(2,1)} %param.14) | copy-start | bytes 786436
  89.1 60.1 %copy-start.12 = (bf16[1024,32]{1,0:T(8,128)(2,1)S(1)}, bf16[1024,32]{1,0:T(8,128)(2,1)}, u32[]{:S(2)}) copy-start(bf16[1024,32]{1,0:T(8,128)(2,1)} %copy-done.11) | copy-start | bytes 196612
  116.3 26.2 %collective-permute-start.9 = (bf16[384,1024]{1,0:T(8,128)(2,1)}, bf16[384,1024]{1,0:T(8,128)(2,1)}, u32[]{:S(2)}, u32[]{:S(2)}) collective-permute-start(bf16[384,1024]{1,0:T(8,128)(2,1)} %constant_dynamic-update-slice_fusion.2.piece0), channel_id=1, source_target_pairs={{0,2},{2,0},{1,3},{3,1},{4,6},{6,4},{5,7},{7,5},{8,10},{10,8},{9,1... | collective-permute-start | bytes 2359304 | tf_op jit(solution)/shard_map/ppermute | solution.py:46
  117.0 22.5 %collective-permute-start.7 = (bf16[256,1024]{1,0:T(8,128)(2,1)}, bf16[256,1024]{1,0:T(8,128)(2,1)}, u32[]{:S(2)}, u32[]{:S(2)}) collective-permute-start(bf16[256,1024]{1,0:T(8,128)(2,1)} %refs_8_.1), channel_id=1, source_target_pairs={{0,1},{1,0},{2,3},{3,2},{4,5},{5,4},{6,7},{7,6},{8,9},{9,8},{10,11... | collective-permute-start | bytes 1572872 | tf_op jit(solution)/shard_map/ppermute | solution.py:46
  117.0 22.5 %collective-permute-start.8 = (bf16[256,1024]{1,0:T(8,128)(2,1)S(1)}, bf16[256,1024]{1,0:T(8,128)(2,1)}, u32[]{:S(2)}, u32[]{:S(2)}) collective-permute-start(bf16[256,1024]{1,0:T(8,128)(2,1)S(1)} %collective-permute-done.6.refs_5_.refs_4_.refs_10_), channel_id=1, source_target_pairs={{0,1},{1,0},{2,3},{3,2},{4,5},{5,4},{6,7},{7,6},{8,9},{9,8},{10,11... | collective-permute-start | bytes 1572872 | tf_op jit(solution)/shard_map/ppermute | solution.py:46
  132.9 16.2 %all-to-all-start.2 = ((bf16[8,128,128]{2,1,0:T(8,128)(2,1)}), bf16[8,128,128]{2,1,0:T(8,128)(2,1)}, u32[]{:S(2)}, u32[]{:S(2)}) async-start(bf16[8,128,128]{2,1,0:T(8,128)(2,1)} %bitcast.15), calls=%async_computation.2 | async-start | bytes 524288 | tf_op jit(solution)/shard_map/all_to_all | solution.py:58
  157.5 48.3 %all-to-all-start.3 = ((bf16[32,48,1024]{2,1,0:T(8,128)(2,1)}), bf16[32,48,1024]{2,1,0:T(8,128)(2,1)}, u32[]{:S(2)}, u32[]{:S(2)}) async-start(bf16[32,48,1024]{2,1,0:T(8,128)(2,1)} %bitcast.93), calls=%async_computation.3 | async-start | bytes 6291456 | tf_op jit(solution)/shard_map/all_to_all | solution.py:58
  164.5 5.4 %collective-permute-start.10 = (bf16[384,1024]{1,0:T(8,128)(2,1)}, bf16[384,1024]{1,0:T(8,128)(2,1)}, u32[]{:S(2)}, u32[]{:S(2)}) collective-permute-start(bf16[384,1024]{1,0:T(8,128)(2,1)} %constant_dynamic-update-slice_fusion.2.piece0), channel_id=1, source_target_pairs={{0,1},{1,0},{2,3},{3,2},{4,5},{5,4},{6,7},{7,6},{8,9},{9,8},{10,11... | collective-permute-start | bytes 2359304 | tf_op jit(solution)/shard_map/ppermute | solution.py:46
  164.8 5.1 %collective-permute-start.11 = (bf16[384,1024]{1,0:T(8,128)(2,1)}, bf16[384,1024]{1,0:T(8,128)(2,1)}, u32[]{:S(2)}, u32[]{:S(2)}) collective-permute-start(bf16[384,1024]{1,0:T(8,128)(2,1)} %collective-permute-done.9.refs_11_.piece2), channel_id=1, source_target_pairs={{0,1},{1,0},{2,3},{3,2},{4,5},{5,4},{6,7},{7,6},{8,9},{9,8},{10,11... | collective-permute-start | bytes 2359304 | tf_op jit(solution)/shard_map/ppermute | solution.py:46
  168.3 65.3 %collective-permute-start.12 = (bf16[256,2048]{1,0:T(8,128)(2,1)}, bf16[256,2048]{1,0:T(8,128)(2,1)}, u32[]{:S(2)}, u32[]{:S(2)}) collective-permute-start(bf16[256,2048]{1,0:T(8,128)(2,1)} %constant_dynamic-update-slice_fusion.1.refs_13_.refs_2_), channel_id=1, source_target_pairs={{0,2},{2,0},{1,3},{3,1},{4,6},{6,4},{5,7},{7,5},{8,10},{10,8},{9,1... | collective-permute-start | bytes 3145736 | tf_op jit(solution)/shard_map/ppermute | solution.py:46
  225.0 54.4 %all-to-all-start.4 = ((bf16[32,48,1152]{2,1,0:T(8,128)(2,1)}), bf16[32,48,1152]{2,1,0:T(8,128)(2,1)}, u32[]{:S(2)}, u32[]{:S(2)}) async-start(bf16[32,48,1152]{2,1,0:T(8,128)(2,1)} %bitcast.91), calls=%async_computation.4 | async-start | bytes 7077888 | tf_op jit(solution)/shard_map/all_to_all | solution.py:58
  235.1 11.7 %copy-start.50 = (s32[128,32]{0,1:T(8,128)S(1)}, s32[128,32]{0,1:T(8,128)}, u32[]{:S(2)}) copy-start(s32[128,32]{0,1:T(8,128)} %copy-done.49) | copy-start | bytes 49156
  246.3 5.0 %collective-permute-start.13 = (bf16[2,384,1024]{2,1,0:T(8,128)(2,1)}, bf16[2,384,1024]{2,1,0:T(8,128)(2,1)}, u32[]{:S(2)}, u32[]{:S(2)}) collective-permute-start(bf16[2,384,1024]{2,1,0:T(8,128)(2,1)} %get-tuple-element.89), channel_id=1, source_target_pairs={{0,1},{1,0},{2,3},{3,2},{4,5},{5,4},{6,7},{7,6},{8,9},{9,8},{10,11... | collective-permute-start | bytes 4718600 | tf_op jit(solution)/shard_map/ppermute | solution.py:46
  246.3 8.9 %collective-permute-start.14 = (bf16[256,2048]{1,0:T(8,128)(2,1)}, bf16[256,2048]{1,0:T(8,128)(2,1)}, u32[]{:S(2)}, u32[]{:S(2)}) collective-permute-start(bf16[256,2048]{1,0:T(8,128)(2,1)} %constant_dynamic-update-slice_fusion.1.refs_13_.refs_2_), channel_id=1, source_target_pairs={{0,1},{1,0},{2,3},{3,2},{4,5},{5,4},{6,7},{7,6},{8,9},{9,8},{10,11... | collective-permute-start | bytes 3145736 | tf_op jit(solution)/shard_map/ppermute | solution.py:46
  246.8 8.4 %collective-permute-start.15 = (bf16[256,2048]{1,0:T(8,128)(2,1)}, bf16[256,2048]{1,0:T(8,128)(2,1)}, u32[]{:S(2)}, u32[]{:S(2)}) collective-permute-start(bf16[256,2048]{1,0:T(8,128)(2,1)} %collective-permute-done.12.refs_5_.refs_15_.refs_4_), channel_id=1, source_target_pairs={{0,1},{1,0},{2,3},{3,2},{4,5},{5,4},{6,7},{7,6},{8,9},{9,8},{10,11... | collective-permute-start | bytes 3145736 | tf_op jit(solution)/shard_map/ppermute | solution.py:46
  251.3 28.2 %copy-start = (bf16[128,1536]{1,0:T(8,128)(2,1)}, bf16[128,1536]{1,0:T(8,128)(2,1)S(1)}, u32[]{:S(2)}) copy-start(bf16[128,1536]{1,0:T(8,128)(2,1)S(1)} %compare_convert_fusion.refs_1_) | copy-start | bytes 1179652
  251.3 28.1 %copy-start.13 = (bf16[1024,32]{1,0:T(8,128)(2,1)S(1)}, bf16[1024,32]{1,0:T(8,128)(2,1)}, u32[]{:S(2)}) copy-start(bf16[1024,32]{1,0:T(8,128)(2,1)} %copy-done.11) | copy-start | bytes 196612
  282.3 4.6 copy-start.34
  282.3 4.6 copy-start.36
  288.7 15.3 %collective-permute-start.19 = (bf16[2,256,1152]{2,1,0:T(8,128)(2,1)S(1)}, bf16[2,256,1152]{2,1,0:T(8,128)(2,1)}, u32[]{:S(2)}, u32[]{:S(2)}) collective-permute-start(bf16[2,256,1152]{2,1,0:T(8,128)(2,1)S(1)} %get-tuple-element.103), channel_id=1, source_target_pairs={{0,1},{1,0},{2,3},{3,2},{4,5},{5,4},{6,7},{7,6},{8,9},{9,8},{10,11... | collective-permute-start | bytes 3538952 | tf_op jit(solution)/shard_map/ppermute | solution.py:46
  298.3 15.2 %all-to-all-start.5 = ((bf16[8,128,128]{2,1,0:T(8,128)(2,1)}), bf16[8,128,128]{2,1,0:T(8,128)(2,1)}, u32[]{:S(2)}, u32[]{:S(2)}) async-start(bf16[8,128,128]{2,1,0:T(8,128)(2,1)} %copy-done.23), calls=%async_computation.5 | async-start | bytes 524288 | tf_op jit(solution)/shard_map/all_to_all | solution.py:58
  304.0 9.5 %copy-start.38 = (s32[16]{0:T(128)S(1)}, s32[16]{0:T(128)}, u32[]{:S(2)}) copy-start(s32[16]{0:T(128)} %copy-done.37) | copy-start | bytes 196
  306.8 35.9 %collective-permute-start.20 = (bf16[256,1152]{1,0:T(8,128)(2,1)}, bf16[256,1152]{1,0:T(8,128)(2,1)}, u32[]{:S(2)}, u32[]{:S(2)}) collective-permute-start(bf16[256,1152]{1,0:T(8,128)(2,1)} %dynamic-slice_bitcast_fusion.1), channel_id=1, source_target_pairs={{0,2},{2,0},{1,3},{3,1},{4,6},{6,4},{5,7},{7,5},{8,10},{10,8},{9,1... | collective-permute-start | bytes 1769480 | tf_op jit(solution)/shard_map/ppermute | solution.py:46
  337.6 17.9 %collective-permute-start.16 = (bf16[1024,128]{1,0:T(8,128)(2,1)S(1)}, bf16[1024,128]{1,0:T(8,128)(2,1)S(1)}, u32[]{:S(2)}, u32[]{:S(2)}) collective-permute-start(bf16[1024,128]{1,0:T(8,128)(2,1)S(1)} %get-tuple-element.95), channel_id=1, source_target_pairs={{0,96},{32,0},{64,32},{96,64},{1,97},{33,1},{65,33},{97,65},{2,98}... | collective-permute-start | bytes 786440 | tf_op jit(solution)/shard_map/ppermute | solution.py:50
  341.7 17.6 %collective-permute-start.17 = (bf16[1024,128]{1,0:T(8,128)(2,1)S(1)}, bf16[1024,128]{1,0:T(8,128)(2,1)S(1)}, u32[]{:S(2)}, u32[]{:S(2)}) collective-permute-start(bf16[1024,128]{1,0:T(8,128)(2,1)S(1)} %get-tuple-element.96), channel_id=1, source_target_pairs={{0,64},{32,96},{64,0},{96,32},{1,65},{33,97},{65,1},{97,33},{2,66}... | collective-permute-start | bytes 786440 | tf_op jit(solution)/shard_map/ppermute | solution.py:50
  341.9 17.4 %collective-permute-start.18 = (bf16[1024,128]{1,0:T(8,128)(2,1)S(1)}, bf16[1024,128]{1,0:T(8,128)(2,1)S(1)}, u32[]{:S(2)}, u32[]{:S(2)}) collective-permute-start(bf16[1024,128]{1,0:T(8,128)(2,1)S(1)} %get-tuple-element.97), channel_id=1, source_target_pairs={{0,32},{32,64},{64,96},{96,0},{1,33},{33,65},{65,97},{97,1},{2,34}... | collective-permute-start | bytes 786440 | tf_op jit(solution)/shard_map/ppermute | solution.py:50
  344.1 16.4 %collective-permute-start.21 = (bf16[64,1152]{1,0:T(8,128)(2,1)S(1)}, bf16[64,1152]{1,0:T(8,128)(2,1)S(1)}, u32[]{:S(2)}, u32[]{:S(2)}) collective-permute-start(bf16[64,1152]{1,0:T(8,128)(2,1)S(1)} %get-tuple-element.105), channel_id=1, source_target_pairs={{0,32},{32,64},{64,96},{96,0},{1,33},{33,65},{65,97},{97,1},{2,34}... | collective-permute-start | bytes 442376 | tf_op jit(solution)/shard_map/ppermute | solution.py:50
  346.7 15.8 %collective-permute-start.22 = (bf16[64,1152]{1,0:T(8,128)(2,1)S(1)}, bf16[64,1152]{1,0:T(8,128)(2,1)S(1)}, u32[]{:S(2)}, u32[]{:S(2)}) collective-permute-start(bf16[64,1152]{1,0:T(8,128)(2,1)S(1)} %get-tuple-element.106), channel_id=1, source_target_pairs={{0,64},{32,96},{64,0},{96,32},{1,65},{33,97},{65,1},{97,33},{2,66}... | collective-permute-start | bytes 442376 | tf_op jit(solution)/shard_map/ppermute | solution.py:50
  355.6 6.9 %collective-permute-start.23 = (bf16[64,1152]{1,0:T(8,128)(2,1)S(1)}, bf16[64,1152]{1,0:T(8,128)(2,1)S(1)}, u32[]{:S(2)}, u32[]{:S(2)}) collective-permute-start(bf16[64,1152]{1,0:T(8,128)(2,1)S(1)} %get-tuple-element.107), channel_id=1, source_target_pairs={{0,96},{32,0},{64,32},{96,64},{1,97},{33,1},{65,33},{97,65},{2,98}... | collective-permute-start | bytes 442376 | tf_op jit(solution)/shard_map/ppermute | solution.py:50
  364.9 20.1 %copy-start.18 = (f32[128,1024]{1,0:T(8,128)S(1)}, f32[128,1024]{1,0:T(8,128)}, u32[]{:S(2)}) copy-start(f32[128,1024]{1,0:T(8,128)} %copy-done.17) | copy-start | bytes 1572868
  365.0 5.0 %collective-permute-start.24 = (bf16[2,256,256]{2,1,0:T(8,128)(2,1)S(1)}, bf16[2,256,256]{2,1,0:T(8,128)(2,1)S(1)}, u32[]{:S(2)}, u32[]{:S(2)}) collective-permute-start(bf16[2,256,256]{2,1,0:T(8,128)(2,1)S(1)} %get-tuple-element.110), channel_id=1, source_target_pairs={{0,1},{1,0},{2,3},{3,2},{4,5},{5,4},{6,7},{7,6},{8,9},{9,8},{10,11... | collective-permute-start | bytes 786440 | tf_op jit(solution)/shard_map/ppermute | solution.py:46
  365.0 20.0 %all-to-all-start.6 = ((bf16[8,176,256]{2,1,0:T(8,128)(2,1)}), bf16[8,176,256]{2,1,0:T(8,128)(2,1)S(1)}, u32[]{:S(2)}, u32[]{:S(2)}) async-start(bf16[8,176,256]{2,1,0:T(8,128)(2,1)} %get-tuple-element.111), calls=%async_computation.6 | async-start | bytes 1441792 | tf_op jit(solution)/shard_map/all_to_all | solution.py:58
  370.1 22.0 %collective-permute-start.25 = (bf16[256,256]{1,0:T(8,128)(2,1)S(1)}, bf16[256,256]{1,0:T(8,128)(2,1)S(1)}, u32[]{:S(2)}, u32[]{:S(2)}) collective-permute-start(bf16[256,256]{1,0:T(8,128)(2,1)S(1)} %dynamic-slice_bitcast_fusion.2), channel_id=1, source_target_pairs={{0,2},{2,0},{1,3},{3,1},{4,6},{6,4},{5,7},{7,5},{8,10},{10,8},{9,1... | collective-permute-start | bytes 393224 | tf_op jit(solution)/shard_map/ppermute | solution.py:46
  389.8 2.3 collective-permute-start.26
  389.8 3.7 collective-permute-start.27
  391.9 3.0 collective-permute-start.28
  397.2 6.2 %copy-start.44 = (bf16[2,384,1024]{2,1,0:T(8,128)(2,1)S(1)}, bf16[2,384,1024]{2,1,0:T(8,128)(2,1)}, u32[]{:S(2)}) copy-start(bf16[2,384,1024]{2,1,0:T(8,128)(2,1)} %add_convert_fusion.refs_12_) | copy-start | bytes 4718596
  397.2 60.7 %all-to-all-start.7 = ((bf16[32,48,1024]{2,1,0:T(8,128)(2,1)}), bf16[32,48,1024]{2,1,0:T(8,128)(2,1)}, u32[]{:S(2)}, u32[]{:S(2)}) async-start(bf16[32,48,1024]{2,1,0:T(8,128)(2,1)} %bitcast.92), calls=%async_computation.7 | async-start | bytes 6291456 | tf_op jit(solution)/shard_map/all_to_all | solution.py:58
  403.5 54.4 %collective-permute-start.32 = (bf16[384,1024]{1,0:T(8,128)(2,1)S(1)}, bf16[384,1024]{1,0:T(8,128)(2,1)S(1)}, u32[]{:S(2)}, u32[]{:S(2)}) collective-permute-start(bf16[384,1024]{1,0:T(8,128)(2,1)S(1)} %dynamic-slice_bitcast_fusion), channel_id=1, source_target_pairs={{0,2},{2,0},{1,3},{3,1},{4,6},{6,4},{5,7},{7,5},{8,10},{10,8},{9,1... | collective-permute-start | bytes 2359304 | tf_op jit(solution)/shard_map/ppermute | solution.py:46
  403.6 43.9 %collective-permute-start.29 = (bf16[80,1152]{1,0:T(8,128)(2,1)S(1)}, bf16[80,1152]{1,0:T(8,128)(2,1)S(1)}, u32[]{:S(2)}, u32[]{:S(2)}) collective-permute-start(bf16[80,1152]{1,0:T(8,128)(2,1)S(1)} %shard_map.245.refs_1_), channel_id=1, source_target_pairs={{0,32},{32,64},{64,96},{96,0},{1,33},{33,65},{65,97},{97,1},{2,34}... | collective-permute-start | bytes 552968 | tf_op jit(solution)/shard_map/ppermute | solution.py:50
  405.4 47.6 %collective-permute-start.30 = (bf16[80,1152]{1,0:T(8,128)(2,1)S(1)}, bf16[80,1152]{1,0:T(8,128)(2,1)S(1)}, u32[]{:S(2)}, u32[]{:S(2)}) collective-permute-start(bf16[80,1152]{1,0:T(8,128)(2,1)S(1)} %shard_map.245.refs_1_), channel_id=1, source_target_pairs={{0,64},{32,96},{64,0},{96,32},{1,65},{33,97},{65,1},{97,33},{2,66}... | collective-permute-start | bytes 552968 | tf_op jit(solution)/shard_map/ppermute | solution.py:50
  408.1 45.0 %collective-permute-start.31 = (bf16[80,1152]{1,0:T(8,128)(2,1)S(1)}, bf16[80,1152]{1,0:T(8,128)(2,1)S(1)}, u32[]{:S(2)}, u32[]{:S(2)}) collective-permute-start(bf16[80,1152]{1,0:T(8,128)(2,1)S(1)} %shard_map.245.refs_1_), channel_id=1, source_target_pairs={{0,96},{32,0},{64,32},{96,64},{1,97},{33,1},{65,33},{97,65},{2,98}... | collective-permute-start | bytes 552968 | tf_op jit(solution)/shard_map/ppermute | solution.py:50
  459.4 9.4 %copy-start.22 = (f32[128,32]{1,0:T(8,128)S(1)}, f32[128,32]{1,0:T(8,128)}, u32[]{:S(2)}) copy-start(f32[128,32]{1,0:T(8,128)} %copy-done.20) | copy-start | bytes 49156
  459.4 33.4 %all-to-all-start.8 = ((bf16[8,96,1152]{2,1,0:T(8,128)(2,1)}), bf16[8,96,1152]{2,1,0:T(8,128)(2,1)S(1)}, u32[]{:S(2)}, u32[]{:S(2)}) async-start(bf16[8,96,1152]{2,1,0:T(8,128)(2,1)} %shard_map.246), calls=%async_computation.8 | async-start | bytes 3538944 | tf_op jit(solution)/shard_map/all_to_all | solution.py:58
  (35 other events, 40.4 us)
